TPU v7x, 32 devices: a whole 2x2x4 slice. The times are simulated.
32 devices in a mesh: seq: 8 (over z, core), tp: 4 (over y, x).
Axes of the slice: x: 2, y: 2, z: 4, core: 2. Of those that a mesh axis runs over, the one named last changes fastest.
Arguments:
- hidden_in: bfloat16 [3072, 3584], P('seq'), may hold values from -48 to 48
- joined_inputs: bfloat16 [3072, 8192], P('seq', 'tp'), may hold values from -64 to 64
- lengths: int32 [4], replicated, may hold values from 1 to 1536, 3072 in all
- o_weight: bfloat16 [4096, 3584], P('tp'), may hold values from -0.09375 to 0.09375
- gate_up: float32 [2, 3584, 7168], P(None, ('seq', 'tp')), may hold values from -0.09375 to 0.09375
- down_weight: bfloat16 [7168, 3584], P('tp'), may hold values from -0.0625 to 0.0625
- next_weight: bfloat16 [3584, 8192], P(None, 'tp'), may hold values from -0.09375 to 0.09375
- post_attn_gain: float32 [3584], replicated, may hold values from 0.1 to 1.9
- pre_ffw_gain: float32 [3584], replicated, may hold values from 0.1 to 1.9
- post_ffw_gain: float32 [3584], replicated, may hold values from 0.1 to 1.9
- next_gain: float32 [3584], replicated, may hold values from 0.1 to 1.9
Outputs:
- next_qkv: bfloat16 [3072, 8192], P('seq', 'tp')
Inputs may be any that keep to these rules, and one draw needn't show every extreme that they name: The lengths of 4 prompts laid end to end; they sum to 3072 and the longest is exactly 1536.
All inputs are finite; a program needn't handle non-finite values.
Results may differ from a plain program's by a relative error of at most 0.022.
Values may be sent and summed in bfloat16 or wider, within the bound.
No kernel may reach another device: no remote copies, remote signals or barrier semaphores. Data moves between devices by JAX's collectives and lax.ppermute only.
A program may use at most 192 MiB of HBM per device.

v0:
```python
import functools

import jax
import jax.numpy as jnp
from jax import lax
from jax.experimental import pallas as pl
from jax.experimental.pallas import tpu as pltpu
from jax.sharding import PartitionSpec as P

HEADS = 16
KV_HEADS = 8
HEAD_DIM = 256
PER_GROUP = HEADS // KV_HEADS
GROUP_COLS = (PER_GROUP + 2) * HEAD_DIM
MIB = 1 << 20
UNIT = 20_000_000_000
CA = 0.1
CM = 4.0
CC = 1.0
CW = 1.0


def span(units):
    return pl.CostEstimate(flops=int(units * UNIT) + 1, bytes_accessed=1000, transcendentals=0)


COST = span(0)


def rms_norm(values, gain):
    meansq = jnp.mean(values * values, axis=-1, keepdims=True)
    return values * lax.rsqrt(meansq + 1e-06) * gain


def tp_swap(values, bits):
    size = lax.axis_size("tp")
    return lax.ppermute(values, "tp", [(i, i ^ bits) for i in range(size)])


def seq_swap(values, bits):
    size = lax.axis_size("seq")
    return lax.ppermute(values, "seq", [(i, i ^ bits) for i in range(size)])


def seq_up(values):
    size = lax.axis_size("seq")
    return lax.ppermute(values, "seq", [(i, i + 2) for i in range(size - 2)])


def after(values, token):
    return lax.optimization_barrier((values, token))[0]


def hint(values):
    return seq_swap(values[:16, :128], 1)


def attention_kernel(ends_ref, place_ref, joined_ref, o_hbm, *refs, blocks, groups, prompts, parts):
    kv_refs = refs[: blocks * groups]
    out_refs = refs[blocks * groups : blocks * groups + parts]
    mark_ref, peak, total, acc, projected, o_ref, sems = refs[blocks * groups + parts :]
    rows = joined_ref.shape[0]
    piece = rows // parts
    head_cols = PER_GROUP * HEAD_DIM
    fetches = []
    for g in range(groups):
        held = pl.ds(g * head_cols, head_cols)
        fetches.append(pltpu.make_async_copy(o_hbm.at[held], o_ref.at[held], sems.at[g]))
        fetches[-1].start()
    first = place_ref[1]
    stacked = PER_GROUP * rows
    at = first + lax.rem(lax.broadcasted_iota(jnp.int32, (stacked, 1), 0), rows)
    start = jnp.zeros_like(at)
    lowest = jnp.int32(0)
    for p in range(prompts):
        end = ends_ref[p]
        start = jnp.where(at >= end, jnp.maximum(start, end), start)
        lowest = jnp.where(first >= end, jnp.maximum(lowest, end), lowest)

    for g in range(groups):
        col = g * GROUP_COLS
        queries = jnp.concatenate(
            [
                joined_ref[:, col + r * HEAD_DIM : col + (r + 1) * HEAD_DIM]
                for r in range(PER_GROUP)
            ],
            axis=0,
        )

        def scores_of(keys, base, queries=queries):
            scores = lax.dot_general(
                queries, keys, (((1,), (1,)), ((), ())), preferred_element_type=jnp.float32
            ) * (HEAD_DIM ** (-0.5))
            places = base + lax.broadcasted_iota(jnp.int32, (1, rows), 1)
            return jnp.where((places >= start) & (places <= at), scores, -1e30)

        own_keys = joined_ref[:, col + head_cols : col + head_cols + HEAD_DIM]
        own_values = joined_ref[:, col + head_cols + HEAD_DIM : col + GROUP_COLS]
        scores = scores_of(own_keys, first)
        top = jnp.max(scores, axis=1, keepdims=True)
        weights = jnp.exp(scores - top)
        peak[...] = jnp.broadcast_to(top, peak.shape)
        total[...] = jnp.broadcast_to(jnp.sum(weights, axis=1, keepdims=True), total.shape)
        acc[...] = jnp.dot(
            weights.astype(jnp.bfloat16), own_values, preferred_element_type=jnp.float32
        )
        for i in range(blocks):
            base = place_ref[2 + i]
            kv_ref = kv_refs[i * groups + g]

            @pl.when((base >= 0) & (base + rows > lowest) & (base < first))
            def _(base=base, kv_ref=kv_ref, scores_of=scores_of):
                scores = scores_of(kv_ref[:, :HEAD_DIM], base)
                before = peak[:, :1]
                top = jnp.maximum(before, jnp.max(scores, axis=1, keepdims=True))
                weights = jnp.exp(scores - top)
                shrink = jnp.exp(before - top)
                peak[...] = jnp.broadcast_to(top, peak.shape)
                total[...] = total[...] * shrink + jnp.sum(weights, axis=1, keepdims=True)
                acc[...] = acc[...] * shrink + jnp.dot(
                    weights.astype(jnp.bfloat16),
                    kv_ref[:, HEAD_DIM:],
                    preferred_element_type=jnp.float32,
                )

        result = (acc[...] / total[:, :1]).astype(jnp.bfloat16)
        attended = jnp.concatenate(
            [result[r * rows : (r + 1) * rows] for r in range(PER_GROUP)], axis=1
        )
        fetches[g].wait()
        tile = 512
        for j in range(o_ref.shape[1] // tile):
            cut = slice(j * tile, (j + 1) * tile)
            product = jnp.dot(
                attended,
                o_ref[g * head_cols : (g + 1) * head_cols, cut],
                preferred_element_type=jnp.float32,
            )
            if g > 0:
                product = product + projected[:, cut]
            projected[:, cut] = product

    for k in range(parts):
        at_row = pl.multiple_of((place_ref[0] ^ k) * piece, piece)
        out_refs[k][...] = projected[pl.ds(at_row, piece)].astype(jnp.bfloat16)
    mark_ref[...] = projected[:16, :128].astype(jnp.bfloat16)


def attend(joined, o_weight, kv_blocks, bases, ends, tp_index, first, parts):
    rows, cols = joined.shape
    width = o_weight.shape[1]
    groups = cols // GROUP_COLS
    place = jnp.stack([tp_index, first] + bases).astype(jnp.int32)
    count = len(kv_blocks)
    stacked = PER_GROUP * rows
    return pl.pallas_call(
        functools.partial(
            attention_kernel, blocks=count, groups=groups, prompts=ends.shape[0], parts=parts
        ),
        in_specs=[pl.BlockSpec(memory_space=pltpu.SMEM)] * 2
        + [pl.BlockSpec(memory_space=pltpu.VMEM), pl.BlockSpec(memory_space=pl.ANY)]
        + [pl.BlockSpec(memory_space=pltpu.VMEM)] * (count * groups),
        out_specs=[pl.BlockSpec(memory_space=pltpu.VMEM)] * (parts + 1),
        scratch_shapes=[
            pltpu.VMEM((stacked, 128), jnp.float32),
            pltpu.VMEM((stacked, 128), jnp.float32),
            pltpu.VMEM((stacked, HEAD_DIM), jnp.float32),
            pltpu.VMEM((rows, width), jnp.float32),
            pltpu.VMEM(o_weight.shape, jnp.bfloat16),
            pltpu.SemaphoreType.DMA((groups,)),
        ],
        out_shape=[jax.ShapeDtypeStruct((rows // parts, width), jnp.bfloat16)] * parts
        + [jax.ShapeDtypeStruct((16, 128), jnp.bfloat16)],
        compiler_params=pltpu.CompilerParams(vmem_limit_bytes=48 * MIB),
        cost_estimate=span(CA),
        name="attention",
    )(ends, place, joined, o_weight, *[kv for block in kv_blocks for kv in block])


def mid_norm_kernel(place_ref, hidden_ref, post_ref, pre_ref, *refs, parts):
    residual_ref, out_ref, *chunk_refs = refs[parts:]
    total = refs[0][...].astype(jnp.float32)
    for k in range(1, parts):
        total = total + refs[k][...].astype(jnp.float32)
    residual = hidden_ref[...].astype(jnp.float32) + rms_norm(total, post_ref[...])
    residual_ref[...] = residual
    result = rms_norm(residual, pre_ref[...]).astype(jnp.bfloat16)
    out_ref[...] = result
    for c, ref in enumerate(chunk_refs):
        ref[...] = result[c * ref.shape[0] : (c + 1) * ref.shape[0]]


def mid_norm(hidden, post_gain, pre_gain, partials, tp_index, chunks):
    parts = len(partials)
    shape = partials[0].shape
    cut = (shape[0] // chunks, shape[1])
    whole = pl.BlockSpec(shape, lambda i, *_: (0, 0))
    gain = pl.BlockSpec((1, shape[1]), lambda i, *_: (0, 0))
    return pl.pallas_call(
        functools.partial(mid_norm_kernel, parts=parts),
        grid_spec=pltpu.PrefetchScalarGridSpec(
            num_scalar_prefetch=1,
            grid=(1,),
            in_specs=[pl.BlockSpec(shape, lambda i, place: (place[0], 0)), gain, gain]
            + [whole] * parts,
            out_specs=[whole, whole] + [pl.BlockSpec(cut, lambda i, *_: (0, 0))] * chunks,
        ),
        out_shape=[
            jax.ShapeDtypeStruct(shape, jnp.float32),
            jax.ShapeDtypeStruct(shape, jnp.bfloat16),
        ]
        + [jax.ShapeDtypeStruct(cut, jnp.bfloat16)] * chunks,
        compiler_params=pltpu.CompilerParams(vmem_limit_bytes=32 * MIB),
        cost_estimate=span(CM),
        name="mid_norm",
    )(tp_index[None].astype(jnp.int32), hidden, post_gain[None], pre_gain[None], *partials)


def out_norm_kernel(residual_ref, post_ref, next_ref, *refs, parts):
    total = refs[0][...].astype(jnp.float32)
    for k in range(1, parts):
        total = total + refs[k][...].astype(jnp.float32)
    residual = residual_ref[...] + rms_norm(total, post_ref[...])
    refs[parts][...] = rms_norm(residual, next_ref[...]).astype(jnp.bfloat16)


def out_norm(residual, post_gain, next_gain, partials, chunk):
    parts = len(partials)
    shape = partials[0].shape
    whole = pl.BlockSpec(shape, lambda i: (0, 0))
    gain = pl.BlockSpec((1, shape[1]), lambda i: (0, 0))
    return pl.pallas_call(
        functools.partial(out_norm_kernel, parts=parts),
        grid=(1,),
        in_specs=[pl.BlockSpec(shape, lambda i: (chunk, 0)), gain, gain] + [whole] * parts,
        out_specs=whole,
        out_shape=jax.ShapeDtypeStruct(shape, jnp.bfloat16),
        compiler_params=pltpu.CompilerParams(vmem_limit_bytes=32 * MIB),
        cost_estimate=COST,
        name="out_norm",
    )(residual, post_gain[None], next_gain[None], *partials)


def hold_kernel(mark_ref, src_ref, out_ref, sems):
    rows = src_ref.shape[0] // sems.shape[0]
    copies = [
        pltpu.make_async_copy(
            src_ref.at[pl.ds(i * rows, rows)], out_ref.at[pl.ds(i * rows, rows)], sems.at[i]
        )
        for i in range(sems.shape[0])
    ]
    for copy in copies:
        copy.start()
    for copy in copies:
        copy.wait()


def hold(weight, mark):
    return pl.pallas_call(
        hold_kernel,
        in_specs=[pl.BlockSpec(memory_space=pl.ANY)] * 2,
        out_specs=pl.BlockSpec(memory_space=pltpu.VMEM),
        out_shape=jax.ShapeDtypeStruct(weight.shape, weight.dtype),
        scratch_shapes=[pltpu.SemaphoreType.DMA((4,))],
        compiler_params=pltpu.CompilerParams(vmem_limit_bytes=18 * MIB),
        cost_estimate=COST,
        name="hold",
    )(mark, weight)


def down_kernel(half_ref, own_ref, returned_ref, w_ref, *refs, parts, chunk):
    x_all = refs[parts]
    rows, hidden = returned_ref.shape
    piece = rows // parts
    for half in range(2):

        @pl.when(half_ref[0] == half)
        def _(half=half):
            x_all[:, half * hidden : (half + 1) * hidden] = own_ref[chunk * rows : (chunk + 1) * rows]
            x_all[:, (1 - half) * hidden : (2 - half) * hidden] = returned_ref[...]

    tile = 512

    @pl.loop(0, w_ref.shape[1] // tile)
    def _(j):
        at = pl.ds(pl.multiple_of(j * tile, tile), tile)
        product = jnp.dot(x_all[...], w_ref[:, at], preferred_element_type=jnp.float32)
        for k in range(parts):
            refs[k][:, at] = product[k * piece : (k + 1) * piece].astype(jnp.bfloat16)


def down(own, returned, weight, half, parts, chunk):
    rows, hidden = returned.shape
    width = weight.shape[1]
    return pl.pallas_call(
        functools.partial(down_kernel, parts=parts, chunk=chunk),
        in_specs=[pl.BlockSpec(memory_space=pltpu.SMEM)]
        + [pl.BlockSpec(memory_space=pltpu.VMEM)] * 3,
        out_specs=[pl.BlockSpec(memory_space=pltpu.VMEM)] * parts,
        scratch_shapes=[pltpu.VMEM((rows, 2 * hidden), jnp.bfloat16)],
        out_shape=[jax.ShapeDtypeStruct((rows // parts, width), jnp.bfloat16)] * parts,
        compiler_params=pltpu.CompilerParams(vmem_limit_bytes=24 * MIB),
        cost_estimate=COST,
        name="down",
    )(half[None].astype(jnp.int32), own, returned, weight)


def next_kernel(place_ref, *refs, parts, chunk):
    x_refs, w_ref = refs[:parts], refs[parts]
    out_ref, x_all, held, sems = refs[-4:]
    piece = x_refs[0].shape[0]
    for k in range(parts):
        x_all[k * piece : (k + 1) * piece] = x_refs[k][...]
    tile = 512
    copies = []
    for j in range(w_ref.shape[1] // tile):
        at = pl.ds(j * tile, tile)
        product = jnp.dot(x_all[...], w_ref[:, at], preferred_element_type=jnp.float32)
        for k in range(parts):
            held[j, k] = product[k * piece : (k + 1) * piece].astype(jnp.bfloat16)
            to = out_ref.at[place_ref[0] ^ k, chunk, :, at]
            copies.append(pltpu.make_async_copy(held.at[j, k], to, sems.at[j * parts + k]))
            copies[-1].start()
    for copy in copies:
        copy.wait()


def next_projection(pieces, weight, tp_index, chunk, chunks, before):
    parts = len(pieces)
    piece, width = pieces[0].shape
    cols = weight.shape[1]
    tile = 512
    operands = [tp_index[None].astype(jnp.int32), *pieces, weight]
    specs = [pl.BlockSpec(memory_space=pltpu.SMEM)]
    specs += [pl.BlockSpec(memory_space=pltpu.VMEM)] * (parts + 1)
    aliases = {}
    if before is not None:
        aliases = {len(operands): 0}
        operands.append(before)
        specs.append(pl.BlockSpec(memory_space=pl.ANY))
    return pl.pallas_call(
        functools.partial(next_kernel, parts=parts, chunk=chunk),
        in_specs=specs,
        out_specs=pl.BlockSpec(memory_space=pl.ANY),
        scratch_shapes=[
            pltpu.VMEM((parts * piece, width), jnp.bfloat16),
            pltpu.VMEM((cols // tile, parts, piece, tile), jnp.bfloat16),
            pltpu.SemaphoreType.DMA((cols // tile * parts,)),
        ],
        out_shape=jax.ShapeDtypeStruct((parts, chunks, piece, cols), jnp.bfloat16),
        input_output_aliases=aliases,
        compiler_params=pltpu.CompilerParams(vmem_limit_bytes=24 * MIB),
        cost_estimate=COST,
        name="next_projection",
    )(*operands)


def pack_kernel(place_ref, *refs, buffers, marks):
    w_refs, (out_ref, sems) = refs[:buffers], refs[buffers + marks :]
    copies = []
    for ref in w_refs:
        for k in range(ref.shape[0]):
            to = pl.multiple_of(place_ref[len(copies)], 16)
            copies.append(
                pltpu.make_async_copy(
                    ref.at[k], out_ref.at[pl.ds(to, ref.shape[1])], sems.at[len(copies)]
                )
            )
            copies[-1].start()
    for copy in copies:
        copy.wait()


def pack(buffers, offsets, depth, marks):
    wide = buffers[0].shape[2]
    return pl.pallas_call(
        functools.partial(pack_kernel, buffers=len(buffers), marks=len(marks)),
        in_specs=[pl.BlockSpec(memory_space=pltpu.SMEM)]
        + [pl.BlockSpec(memory_space=pl.ANY)] * (len(buffers) + len(marks)),
        out_specs=pl.BlockSpec(memory_space=pltpu.VMEM),
        out_shape=jax.ShapeDtypeStruct((depth, wide), jnp.bfloat16),
        scratch_shapes=[pltpu.SemaphoreType.DMA((len(offsets),))],
        compiler_params=pltpu.CompilerParams(vmem_limit_bytes=16 * MIB),
        cost_estimate=COST,
        name="pack",
    )(jnp.stack(offsets).astype(jnp.int32), *buffers, *marks)


def gate_up_kernel(half_ref, *refs, parts, picked, chunks):
    x_refs, w_refs = refs[:parts], refs[parts : parts + 2]
    out_ref, x_all, acc = refs[parts + 2 :]
    piece = x_refs[0].shape[0] // chunks
    half_depth, both = w_refs[0].shape
    hidden = both // 2
    for i, chunk in enumerate(picked):
        for k in range(parts):
            at = (i * parts + k) * piece
            x_all[at : at + piece] = x_refs[k][chunk * piece : (chunk + 1) * piece]
    tile = 256 if both % 256 == 0 else 128
    near = pl.multiple_of(half_ref[0] * half_depth, 128)
    far = pl.multiple_of((1 - half_ref[0]) * half_depth, 128)

    @pl.loop(0, both // tile)
    def _(j):
        at = pl.ds(pl.multiple_of(j * tile, tile), tile)
        acc[:, at] = jnp.dot(
            x_all[:, pl.ds(near, half_depth)], w_refs[0][:, at], preferred_element_type=jnp.float32
        ) + jnp.dot(
            x_all[:, pl.ds(far, half_depth)], w_refs[1][:, at], preferred_element_type=jnp.float32
        )

    out_ref[...] = (
        jax.nn.gelu(acc[:, :hidden], approximate=True) * acc[:, hidden:]
    ).astype(jnp.bfloat16)


def gate_up_act(pieces, picked, chunks, packed, half):
    parts = len(pieces)
    piece, depth = pieces[0].shape
    rows = parts * piece * len(picked) // chunks
    wide = packed[0].shape[1]
    return pl.pallas_call(
        functools.partial(gate_up_kernel, parts=parts, picked=picked, chunks=chunks),
        in_specs=[pl.BlockSpec(memory_space=pltpu.SMEM)]
        + [pl.BlockSpec(memory_space=pltpu.VMEM)] * (parts + 2),
        out_specs=pl.BlockSpec(memory_space=pltpu.VMEM),
        out_shape=jax.ShapeDtypeStruct((rows, wide // 2), jnp.bfloat16),
        scratch_shapes=[
            pltpu.VMEM((rows, depth), jnp.bfloat16),
            pltpu.VMEM((rows, wide), jnp.float32),
        ],
        compiler_params=pltpu.CompilerParams(vmem_limit_bytes=28 * MIB),
        cost_estimate=COST,
        name="gate_up",
    )(half[None].astype(jnp.int32), *pieces, *packed)


def gather_weights(gate_up, tp_index, seq_index):
    seq_count, tp_count = lax.axis_size("seq"), lax.axis_size("tp")
    half_count = seq_count // 2
    half = seq_index // half_count
    piece_rows = gate_up.shape[1]
    units = gate_up.shape[2] // tp_count
    hidden = units // 2
    pieces = []
    for k in range(tp_count):
        cut = lax.dynamic_slice(
            gate_up, (0, 0, (tp_index ^ k) * units), (2, piece_rows, units)
        ).astype(jnp.bfloat16)
        pieces.append(tp_swap(cut, k) if k else cut)

    def columns(which):
        cuts = [lax.dynamic_slice_in_dim(p, which * hidden, hidden, 2) for p in pieces]
        cuts = [jnp.concatenate([cut[0], cut[1]], axis=1) for cut in cuts]
        stack = jnp.stack(cuts)
        ordered = [
            lax.dynamic_index_in_dim(stack, tp_index ^ j, 0, keepdims=False)
            for j in range(tp_count)
        ]
        return jnp.concatenate(ordered, axis=0)[None]

    if piece_rows % 16 == 0:
        low, high = assemble(pieces)
    else:
        low, high = columns(0), columns(1)
    return low, high


def spread_doubling(low, high, half):
    half_count = lax.axis_size("seq") // 2
    mine, other = jnp.where(half == 0, low, high), jnp.where(half == 0, high, low)
    found = {0: mine, half_count: seq_swap(other, half_count)}
    bits = 2
    while bits < half_count:
        for key in list(found):
            found[key ^ bits] = seq_swap(found[key], bits)
        bits *= 2
    for key in list(found):
        found[key ^ 1] = seq_swap(found[key], 1)
    return found


def spread_line(low, high, half, gates, pack_one):
    chip = lax.axis_index("seq") // 2
    upper = half == 1

    def up(values, first, count):
        pairs = [(s, s + 2) for s in range(2 * first, 2 * (first + count))]
        return lax.ppermute(values, "seq", pairs)

    def down(values, first, count):
        pairs = [(s + 2, s) for s in range(2 * first, 2 * (first + count))]
        return lax.ppermute(values, "seq", pairs)

    low, high = after((low, high), gates[0])
    mine = jnp.where(upper, high, low)
    up_one, down_one = up(high, 0, 3), down(low, 0, 3)
    handed, seen_one = lax.optimization_barrier(((up_one, down_one), gates[1]))
    up_two = up(jnp.where(chip == 0, low, handed[0]), 0, 3)
    down_two = down(jnp.where(chip == 3, high, handed[1]), 0, 3)
    up_two, down_two = after((up_two, down_two), gates[2])
    up_three, down_three = up(up_two, 2, 1), down(down_two, 0, 1)
    inner = (chip == 1) | (chip == 2)
    found = {
        0: mine,
        2: jnp.where(
            inner, jnp.where(upper, down_two, up_two), jnp.where(upper, up_one, down_one)
        ),
        4: jnp.where(upper, up_two, down_two),
    }
    for key in list(found):
        found[key ^ 1] = seq_swap(found[key], 1)
    near = pack_one(found, range(4), [seen_one])
    (up_three, down_three), (near, found[5], _) = lax.optimization_barrier(
        ((up_three, down_three), (near, found[5], gates[3]))
    )
    found[6] = jnp.where(
        inner, jnp.where(upper, up_one, down_one), jnp.where(upper, up_three, down_three)
    )
    found[7] = [seq_swap(found[6][k : k + 1], 1) for k in range(found[6].shape[0])]
    return [near, pack_one(found, range(4, 8), [])]


def pack_half(found, keys, depth, piece_rows, tp_index, seq_index, marks):
    tp_count, half_count = lax.axis_size("tp"), lax.axis_size("seq") // 2
    buffers, offsets = [], []
    for key in keys:
        base = ((seq_index ^ key) % half_count) * (tp_count * piece_rows)
        parts = found[key] if isinstance(found[key], list) else [found[key]]
        subs = sum(part.shape[0] for part in parts)
        sub_rows = parts[0].shape[1]
        buffers += parts
        for k in range(subs):
            offsets.append(base + (tp_index ^ k) * sub_rows if subs > 1 else base)
    return pack(buffers, offsets, depth // 2, marks)


def assemble_kernel(*refs, parts):
    piece_refs, out_refs = refs[:parts], refs[parts:]
    hidden = piece_refs[0].shape[2] // 2
    for k in range(parts):
        for half in range(2):
            for m in range(2):
                out_refs[half][k, :, m * hidden : (m + 1) * hidden] = piece_refs[k][
                    m, :, half * hidden : (half + 1) * hidden
                ]


def assemble(pieces):
    parts = len(pieces)
    _, rows, units = pieces[0].shape
    return pl.pallas_call(
        functools.partial(assemble_kernel, parts=parts),
        out_shape=[jax.ShapeDtypeStruct((parts, rows, units), jnp.bfloat16)] * 2,
        compiler_params=pltpu.CompilerParams(vmem_limit_bytes=32 * MIB),
        cost_estimate=span(CW),
        name="assemble",
    )(*pieces)


def tp_scatter(partials):
    return [tp_swap(part, k) if k else part for k, part in enumerate(partials)]


def tp_gather(values, parts):
    return [values] + [tp_swap(values, k) for k in range(1, parts)]


def local(
    hidden_in,
    joined_inputs,
    lengths,
    o_weight,
    gate_up,
    down_weight,
    next_weight,
    post_attn_gain,
    pre_ffw_gain,
    post_ffw_gain,
    next_gain,
):
    seq_count, tp_count = lax.axis_size("seq"), lax.axis_size("tp")
    seq_index, tp_index = lax.axis_index("seq"), lax.axis_index("tp")
    rows = hidden_in.shape[0]
    half_count = seq_count // 2
    groups = joined_inputs.shape[1] // GROUP_COLS

    own_kv = [
        joined_inputs[:, g * GROUP_COLS + PER_GROUP * HEAD_DIM : (g + 1) * GROUP_COLS]
        for g in range(groups)
    ]
    chain = [own_kv]
    for _ in range(seq_count // 4):
        chain.append([seq_up(kv) for kv in chain[-1]])
    other = [[seq_swap(kv, 1) for kv in block] for block in chain]
    blocks, bases = [], []
    for j in range(len(chain)):
        if j:
            blocks.append(chain[j])
            bases.append((seq_index - 2 * j) * rows)
        blocks.append(other[j])
        bases.append(((seq_index ^ 1) - 2 * j) * rows)

    half = seq_index // half_count
    low, high = gather_weights(after(gate_up, own_kv[0]), tp_index, seq_index)

    ends = jnp.cumsum(lengths).astype(jnp.int32)
    *projected, mark = attend(
        joined_inputs, o_weight, blocks, bases, ends, tp_index, seq_index * rows, tp_count
    )
    piece = rows // tp_count
    chunks = 2 if piece % 32 == 0 else 1
    residual_mid, ffw_in, *ffw_in_cuts = mid_norm(
        hidden_in, post_attn_gain, pre_ffw_gain, tp_scatter(projected), tp_index, chunks
    )
    own_pieces = tp_gather(ffw_in, tp_count)
    partner_in = [seq_swap(cut, half_count) for cut in ffw_in_cuts]
    partner_pieces = [tp_gather(cut, tp_count) for cut in partner_in]
    pack_one = lambda found, keys, marks: pack_half(
        found, keys, hidden_in.shape[1], gate_up.shape[1], tp_index, seq_index, marks
    )
    if seq_count == 8:
        gates = [
            chain[-1],
            seq_swap(mark, 1),
            own_pieces[:-1],
            partner_pieces,
        ]
        packed = spread_line(low, high, half, gates, pack_one)
    else:
        found = spread_doubling(low, high, half)
        packed = [pack_one(found, range(at, at + half_count), []) for at in (0, half_count)]
    returned = [
        seq_swap(gate_up_act(pieces, [0], 1, packed, half), half_count)
        for pieces in partner_pieces
    ]
    own_act = gate_up_act(own_pieces, list(range(chunks)), chunks, packed, half)
    down_held = hold(down_weight, partner_pieces[0][0])
    next_held = hold(next_weight, own_act)
    result = None
    gathered = []
    for c in range(chunks):
        ffw_out = down(own_act, returned[c], down_held, half, tp_count, c)
        next_in = out_norm(residual_mid, post_ffw_gain, next_gain, tp_scatter(ffw_out), c)
        gathered.append(tp_gather(next_in, tp_count))
    for c in range(chunks):
        result = next_projection(gathered[c], next_held, tp_index, c, chunks, result)
    return result.reshape(rows, next_weight.shape[1])


def solution(mesh):
    in_specs = (
        P("seq", None),
        P("seq", "tp"),
        P(),
        P("tp", None),
        P(None, ("seq", "tp"), None),
        P("tp", None),
        P(None, "tp"),
        P(),
        P(),
        P(),
        P(),
    )
    out_specs = P("seq", "tp")
    return jax.shard_map(local, mesh=mesh, in_specs=in_specs, out_specs=out_specs, check_vma=False)
```

profile of v0, /device:TPU:0, one launch (start us, length us, event | category | flops | bytes accessed | tf_op | source)
XLA Modules:
  0.0 335.8 jit_solution(84632563936789354)
XLA Ops:
  4.7 4.0 %collective-permute-start.18 = (bf16[2,112,1792]{2,1,0:T(8,128)(2,1)S(1)}, bf16[2,112,1792]{2,1,0:T(8,128)(2,1)S(1)}, u32[]{:S(2)}, u32[]{:S(2)}) collective-permute-start(bf16[2,112,1792]{2,1,0:T(8,128)(2,1)S(1)} %get-tuple-element.67), channel_id=1, source_target_pairs={{0,3},{1,2},{2,1},{3,0},{4,7},{5,6},{6,5},{7,4},{8,11},{9,10},{10,... | collective-permute-start | bytes 2408456 | tf_op jit(solution)/shard_map/ppermute | solution.py:37
  9.3 3.9 %collective-permute-start.3 = (bf16[384,512]{1,0:T(8,128)(2,1)S(1)}, bf16[384,512]{1,0:T(8,128)(2,1)S(1)}, u32[]{:S(2)}, u32[]{:S(2)}) collective-permute-start(bf16[384,512]{1,0:T(8,128)(2,1)S(1)} %get-tuple-element.80), channel_id=1, source_target_pairs={{0,8},{4,12},{8,16},{12,20},{16,24},{20,28},{1,9},{5,13},{9,17},{1... | collective-permute-start | bytes 1179656 | tf_op jit(solution)/shard_map/ppermute | solution.py:47
  13.2 4.3 %collective-permute-start.2 = (bf16[384,512]{1,0:T(8,128)(2,1)S(1)}, bf16[384,512]{1,0:T(8,128)(2,1)}, u32[]{:S(2)}, u32[]{:S(2)}) collective-permute-start(bf16[384,512]{1,0:T(8,128)(2,1)S(1)} %get-tuple-element.81), channel_id=1, source_target_pairs={{0,8},{4,12},{8,16},{12,20},{16,24},{20,28},{1,9},{5,13},{9,17},{1... | collective-permute-start | bytes 1179656 | tf_op jit(solution)/shard_map/ppermute | solution.py:47
  17.4 5.3 %collective-permute-done.3.refs_3_ = bf16[384,512]{1,0:T(8,128)(2,1)S(1)} collective-permute-done((bf16[384,512]{1,0:T(8,128)(2,1)S(1)}, bf16[384,512]{1,0:T(8,128)(2,1)S(1)}, u32[]{:S(2)}, u32[]{:S(2)}) %collective-permute-start.3) | collective-permute-done | bytes 393248 | tf_op jit(solution)/shard_map/ppermute | solution.py:47
  22.7 5.2 %collective-permute-start.7 = (bf16[384,512]{1,0:T(8,128)(2,1)S(1)}, bf16[384,512]{1,0:T(8,128)(2,1)}, u32[]{:S(2)}, u32[]{:S(2)}) collective-permute-start(bf16[384,512]{1,0:T(8,128)(2,1)S(1)} %collective-permute-done.3.refs_3_), channel_id=1, source_target_pairs={{0,8},{4,12},{8,16},{12,20},{16,24},{20,28},{1,9},{5,13},{9,17},{1... | collective-permute-start | bytes 1179656 | tf_op jit(solution)/shard_map/ppermute | solution.py:47
  31.1 5.2 %collective-permute-start.6 = (bf16[384,512]{1,0:T(8,128)(2,1)}, bf16[384,512]{1,0:T(8,128)(2,1)}, u32[]{:S(2)}, u32[]{:S(2)}) collective-permute-start(bf16[384,512]{1,0:T(8,128)(2,1)} %collective-permute-done.2.refs_2_), channel_id=1, source_target_pairs={{0,8},{4,12},{8,16},{12,20},{16,24},{20,28},{1,9},{5,13},{9,17},{1... | collective-permute-start | bytes 1179656 | tf_op jit(solution)/shard_map/ppermute | solution.py:47
  36.4 7.4 %collective-permute-done.17.refs_2_ = bf16[2,112,1792]{2,1,0:T(8,128)(2,1)S(1)} collective-permute-done((bf16[2,112,1792]{2,1,0:T(8,128)(2,1)S(1)}, bf16[2,112,1792]{2,1,0:T(8,128)(2,1)S(1)}, u32[]{:S(2)}, u32[]{:S(2)}) %collective-permute-start.17) | collective-permute-done | bytes 802848 | tf_op jit(solution)/shard_map/ppermute | solution.py:37
  47.3 6.2 %collective-permute-start.19 = (bf16[4,112,1792]{2,1,0:T(8,128)(2,1)S(1)}, bf16[4,112,1792]{2,1,0:T(8,128)(2,1)}, u32[]{:S(2)}, u32[]{:S(2)}) collective-permute-start(bf16[4,112,1792]{2,1,0:T(8,128)(2,1)S(1)} %get-tuple-element.46), channel_id=1, source_target_pairs={{0,8},{4,12},{8,16},{12,20},{16,24},{20,28},{1,9},{5,13},{9,17},{1... | collective-permute-start | bytes 4816904 | tf_op jit(solution)/shard_map/ppermute | solution.py:489
  64.1 9.5 %attention.1 = (bf16[96,3584]{1,0:T(8,128)(2,1)S(1)}, bf16[96,3584]{1,0:T(8,128)(2,1)S(1)}, bf16[96,3584]{1,0:T(8,128)(2,1)S(1)}, bf16[96,3584]{1,0:T(8,128)(2,1)}, bf16[16,128]{1,0:T(8,128)(2,1)S(1)}) custom-call(s32[4]{0:T(128)S(1)} %bitcast.45, s32[7]{0:T(128)S(1)} %stack.130.place_ref, bf16[384,2048]{1,0:T(8,128)(2,1)} %joined_ref.1, ...), custom_call_target="tpu_custom_call" | custom-call | flops 2000000000 | bytes 1000 | tf_op jit(solution)/shard_map/attention/pallas_call | solution.py:156
  88.7 6.1 %collective-permute-start.22 = (bf16[4,112,1792]{2,1,0:T(8,128)(2,1)}, bf16[4,112,1792]{2,1,0:T(8,128)(2,1)}, u32[]{:S(2)}, u32[]{:S(2)}) collective-permute-start(bf16[4,112,1792]{2,1,0:T(8,128)(2,1)} %get-tuple-element.78), channel_id=1, source_target_pairs={{0,8},{4,12},{8,16},{12,20},{16,24},{20,28},{1,9},{5,13},{9,17},{1... | collective-permute-start | bytes 4816904 | tf_op jit(solution)/shard_map/ppermute | solution.py:489
  97.7 15.0 %collective-permute-done.11.refs_2_ = bf16[96,3584]{1,0:T(8,128)(2,1)S(1)} collective-permute-done((bf16[96,3584]{1,0:T(8,128)(2,1)}, bf16[96,3584]{1,0:T(8,128)(2,1)S(1)}, u32[]{:S(2)}, u32[]{:S(2)}) %collective-permute-start.11) | collective-permute-done | bytes 688160 | tf_op jit(solution)/shard_map/ppermute | solution.py:37
  117.7 6.4 %collective-permute-start.29 = (bf16[48,3584]{1,0:T(8,128)(2,1)S(1)}, bf16[48,3584]{1,0:T(8,128)(2,1)S(1)}, u32[]{:S(2)}, u32[]{:S(2)}) collective-permute-start(bf16[48,3584]{1,0:T(8,128)(2,1)S(1)} %get-tuple-element.53), channel_id=1, source_target_pairs={{0,16},{4,20},{8,24},{12,28},{16,0},{20,4},{24,8},{28,12},{1,17},{... | collective-permute-start | bytes 1032200 | tf_op jit(solution)/shard_map/ppermute | solution.py:42
  124.1 35.8 %collective-permute-done.29.mark_ref.refs_0_ = bf16[48,3584]{1,0:T(8,128)(2,1)S(1)} collective-permute-done((bf16[48,3584]{1,0:T(8,128)(2,1)S(1)}, bf16[48,3584]{1,0:T(8,128)(2,1)S(1)}, u32[]{:S(2)}, u32[]{:S(2)}) %collective-permute-start.29) | collective-permute-done | bytes 344096 | tf_op jit(solution)/shard_map/ppermute | solution.py:42
  175.1 4.9 %collective-permute-done.31.refs_2_ = bf16[48,3584]{1,0:T(8,128)(2,1)S(1)} collective-permute-done((bf16[48,3584]{1,0:T(8,128)(2,1)S(1)}, bf16[48,3584]{1,0:T(8,128)(2,1)S(1)}, u32[]{:S(2)}, u32[]{:S(2)}) %collective-permute-start.31) | collective-permute-done | bytes 344096 | tf_op jit(solution)/shard_map/ppermute | solution.py:37
  200.6 21.8 %collective-permute-done.25 = bf16[4,112,1792]{2,1,0:T(8,128)(2,1)} collective-permute-done((bf16[4,112,1792]{2,1,0:T(8,128)(2,1)}, bf16[4,112,1792]{2,1,0:T(8,128)(2,1)}, u32[]{:S(2)}, u32[]{:S(2)}) %collective-permute-start.25) | collective-permute-done | bytes 1605664 | tf_op jit(solution)/shard_map/ppermute | solution.py:493
  237.1 4.0 %gate_up.5 = bf16[192,896]{1,0:T(8,128)(2,1)S(1)} custom-call(s32[1]{0:T(128)} %bitcast.9.half_ref, bf16[48,3584]{1,0:T(8,128)(2,1)S(1)} %collective-permute-done.29.mark_ref.refs_0_, bf16[48,3584]{1,0:T(8,128)(2,1)S(1)} %copy-done.34, bf16[48,3584]{1,0:T(8,128)(2,1)S(1)} %copy-done.32, bf16[48,3584]{1,0:T(8,128)(2,1)S(1)} %copy-done.30, ...), custom_call_target="tpu_custom_call" | custom-call | flops 1 | bytes 1000 | tf_op jit(solution)/shard_map/gate_up/pallas_call | solution.py:422
  241.2 4.6 %copy-done.6 = bf16[1792,3584]{1,0:T(8,128)(2,1)S(1)} copy-done((bf16[1792,3584]{1,0:T(8,128)(2,1)S(1)}, bf16[1792,3584]{1,0:T(8,128)(2,1)}, u32[]{:S(2)}) %copy-start.6) | copy-done | bytes 12845080
  248.7 5.3 %gate_up.4 = bf16[192,896]{1,0:T(8,128)(2,1)S(1)} custom-call(s32[1]{0:T(128)} %bitcast.9.half_ref, bf16[48,3584]{1,0:T(8,128)(2,1)} %collective-permute-done.33.refs_0_, bf16[48,3584]{1,0:T(8,128)(2,1)} %collective-permute-done.34.refs_1_, bf16[48,3584]{1,0:T(8,128)(2,1)} %collective-permute-done.35.refs_2_, bf16[48,3584]{1,0:T(8,128)(2,1)S(1)} %copy-done.36, ...), custom_call_target="tpu_custom_call" | custom-call | flops 1 | bytes 1000 | tf_op jit(solution)/shard_map/gate_up/pallas_call | solution.py:422
  257.0 7.9 %gate_up.3.own_ref.mark_ref = bf16[384,896]{1,0:T(8,128)(2,1)S(1)} custom-call(s32[1]{0:T(128)} %bitcast.9.half_ref, bf16[96,3584]{1,0:T(8,128)(2,1)S(1)} %copy-done.16, bf16[96,3584]{1,0:T(8,128)(2,1)S(1)} %copy-done.20, bf16[96,3584]{1,0:T(8,128)(2,1)S(1)} %copy-done.18, bf16[96,3584]{1,0:T(8,128)(2,1)} %collective-permute-done.15.refs_3_, ...), custom_call_target="tpu_custom_call" | custom-call | flops 1 | bytes 1000 | tf_op jit(solution)/shard_map/gate_up/pallas_call | solution.py:422
  273.2 4.0 %down.2 = (bf16[48,3584]{1,0:T(8,128)(2,1)S(1)}, bf16[48,3584]{1,0:T(8,128)(2,1)S(1)}, bf16[48,3584]{1,0:T(8,128)(2,1)S(1)}, bf16[48,3584]{1,0:T(8,128)(2,1)S(1)}) custom-call(s32[1]{0:T(128)} %bitcast.9.half_ref, bf16[384,896]{1,0:T(8,128)(2,1)S(1)} %gate_up.3.own_ref.mark_ref, bf16[192,896]{1,0:T(8,128)(2,1)S(1)} %collective-permute-done.41.returned_ref, ...), custom_call_target="tpu_custom_call" | custom-call | flops 1 | bytes 1000 | tf_op jit(solution)/shard_map/down/pallas_call | solution.py:295
  282.2 5.3 %collective-permute-done.50.refs_2_ = bf16[48,3584]{1,0:T(8,128)(2,1)S(1)} collective-permute-done((bf16[48,3584]{1,0:T(8,128)(2,1)S(1)}, bf16[48,3584]{1,0:T(8,128)(2,1)S(1)}, u32[]{:S(2)}, u32[]{:S(2)}) %collective-permute-start.50) | collective-permute-done | bytes 344096 | tf_op jit(solution)/shard_map/ppermute | solution.py:37
  296.1 13.5 %collective-permute-done.43.refs_2_ = bf16[48,3584]{1,0:T(8,128)(2,1)S(1)} collective-permute-done((bf16[48,3584]{1,0:T(8,128)(2,1)S(1)}, bf16[48,3584]{1,0:T(8,128)(2,1)S(1)}, u32[]{:S(2)}, u32[]{:S(2)}) %collective-permute-start.43) | collective-permute-done | bytes 344096 | tf_op jit(solution)/shard_map/ppermute | solution.py:37
  313.6 5.2 %copy-done.3 = bf16[3584,2048]{1,0:T(8,128)(2,1)S(1)} copy-done((bf16[3584,2048]{1,0:T(8,128)(2,1)S(1)}, bf16[3584,2048]{1,0:T(8,128)(2,1)}, u32[]{:S(2)}) %copy-start.3) | copy-done | bytes 14680088
  319.8 4.5 %collective-permute-done.53.refs_2_ = bf16[48,3584]{1,0:T(8,128)(2,1)S(1)} collective-permute-done((bf16[48,3584]{1,0:T(8,128)(2,1)S(1)}, bf16[48,3584]{1,0:T(8,128)(2,1)S(1)}, u32[]{:S(2)}, u32[]{:S(2)}) %collective-permute-start.53) | collective-permute-done | bytes 344096 | tf_op jit(solution)/shard_map/ppermute | solution.py:37
  (229 shorter events, 139.6 us)
Async XLA Ops:
  4.7 31.7 %collective-permute-start.18 = (bf16[2,112,1792]{2,1,0:T(8,128)(2,1)S(1)}, bf16[2,112,1792]{2,1,0:T(8,128)(2,1)S(1)}, u32[]{:S(2)}, u32[]{:S(2)}) collective-permute-start(bf16[2,112,1792]{2,1,0:T(8,128)(2,1)S(1)} %get-tuple-element.67), channel_id=1, source_target_pairs={{0,3},{1,2},{2,1},{3,0},{4,7},{5,6},{6,5},{7,4},{8,11},{9,10},{10,... | collective-permute-start | bytes 2408456 | tf_op jit(solution)/shard_map/ppermute | solution.py:37
  8.6 35.1 %collective-permute-start.17 = (bf16[2,112,1792]{2,1,0:T(8,128)(2,1)S(1)}, bf16[2,112,1792]{2,1,0:T(8,128)(2,1)S(1)}, u32[]{:S(2)}, u32[]{:S(2)}) collective-permute-start(bf16[2,112,1792]{2,1,0:T(8,128)(2,1)S(1)} %get-tuple-element.68), channel_id=1, source_target_pairs={{0,2},{1,3},{2,0},{3,1},{4,6},{5,7},{6,4},{7,5},{8,10},{9,11},{10,... | collective-permute-start | bytes 2408456 | tf_op jit(solution)/shard_map/ppermute | solution.py:37
  9.1 34.9 %collective-permute-start.16 = (bf16[2,112,1792]{2,1,0:T(8,128)(2,1)S(1)}, bf16[2,112,1792]{2,1,0:T(8,128)(2,1)S(1)}, u32[]{:S(2)}, u32[]{:S(2)}) collective-permute-start(bf16[2,112,1792]{2,1,0:T(8,128)(2,1)S(1)} %get-tuple-element.69), channel_id=1, source_target_pairs={{0,1},{1,0},{2,3},{3,2},{4,5},{5,4},{6,7},{7,6},{8,9},{9,8},{10,11... | collective-permute-start | bytes 2408456 | tf_op jit(solution)/shard_map/ppermute | solution.py:37
  22.7 21.6 %collective-permute-start.7 = (bf16[384,512]{1,0:T(8,128)(2,1)S(1)}, bf16[384,512]{1,0:T(8,128)(2,1)}, u32[]{:S(2)}, u32[]{:S(2)}) collective-permute-start(bf16[384,512]{1,0:T(8,128)(2,1)S(1)} %collective-permute-done.3.refs_3_), channel_id=1, source_target_pairs={{0,8},{4,12},{8,16},{12,20},{16,24},{20,28},{1,9},{5,13},{9,17},{1... | collective-permute-start | bytes 1179656 | tf_op jit(solution)/shard_map/ppermute | solution.py:47
  46.0 37.8 %collective-permute-start.20 = (bf16[4,112,1792]{2,1,0:T(8,128)(2,1)S(1)}, bf16[4,112,1792]{2,1,0:T(8,128)(2,1)}, u32[]{:S(2)}, u32[]{:S(2)}) collective-permute-start(bf16[4,112,1792]{2,1,0:T(8,128)(2,1)S(1)} %get-tuple-element.45), channel_id=1, source_target_pairs={{8,0},{12,4},{16,8},{20,12},{24,16},{28,20},{9,1},{13,5},{17,9},{2... | collective-permute-start | bytes 4816904 | tf_op jit(solution)/shard_map/ppermute | solution.py:493
  47.3 37.6 %collective-permute-start.19 = (bf16[4,112,1792]{2,1,0:T(8,128)(2,1)S(1)}, bf16[4,112,1792]{2,1,0:T(8,128)(2,1)}, u32[]{:S(2)}, u32[]{:S(2)}) collective-permute-start(bf16[4,112,1792]{2,1,0:T(8,128)(2,1)S(1)} %get-tuple-element.46), channel_id=1, source_target_pairs={{0,8},{4,12},{8,16},{12,20},{16,24},{20,28},{1,9},{5,13},{9,17},{1... | collective-permute-start | bytes 4816904 | tf_op jit(solution)/shard_map/ppermute | solution.py:489
  80.7 32.0 %collective-permute-start.11 = (bf16[96,3584]{1,0:T(8,128)(2,1)}, bf16[96,3584]{1,0:T(8,128)(2,1)S(1)}, u32[]{:S(2)}, u32[]{:S(2)}) collective-permute-start(bf16[96,3584]{1,0:T(8,128)(2,1)} %copy-done.43), channel_id=1, source_target_pairs={{0,2},{1,3},{2,0},{3,1},{4,6},{5,7},{6,4},{7,5},{8,10},{9,11},{10,... | collective-permute-start | bytes 2064392 | tf_op jit(solution)/shard_map/ppermute | solution.py:37
  82.2 30.5 %collective-permute-start.12 = (bf16[96,3584]{1,0:T(8,128)(2,1)}, bf16[96,3584]{1,0:T(8,128)(2,1)S(1)}, u32[]{:S(2)}, u32[]{:S(2)}) collective-permute-start(bf16[96,3584]{1,0:T(8,128)(2,1)} %get-tuple-element.39), channel_id=1, source_target_pairs={{0,3},{1,2},{2,1},{3,0},{4,7},{5,6},{6,5},{7,4},{8,11},{9,10},{10,... | collective-permute-start | bytes 2064392 | tf_op jit(solution)/shard_map/ppermute | solution.py:37
  88.7 75.2 %collective-permute-start.22 = (bf16[4,112,1792]{2,1,0:T(8,128)(2,1)}, bf16[4,112,1792]{2,1,0:T(8,128)(2,1)}, u32[]{:S(2)}, u32[]{:S(2)}) collective-permute-start(bf16[4,112,1792]{2,1,0:T(8,128)(2,1)} %get-tuple-element.78), channel_id=1, source_target_pairs={{0,8},{4,12},{8,16},{12,20},{16,24},{20,28},{1,9},{5,13},{9,17},{1... | collective-permute-start | bytes 4816904 | tf_op jit(solution)/shard_map/ppermute | solution.py:489
  94.8 70.3 %collective-permute-start.23 = (bf16[4,112,1792]{2,1,0:T(8,128)(2,1)}, bf16[4,112,1792]{2,1,0:T(8,128)(2,1)}, u32[]{:S(2)}, u32[]{:S(2)}) collective-permute-start(bf16[4,112,1792]{2,1,0:T(8,128)(2,1)} %get-tuple-element.79), channel_id=1, source_target_pairs={{8,0},{12,4},{16,8},{20,12},{24,16},{28,20},{9,1},{13,5},{17,9},{2... | collective-permute-start | bytes 4816904 | tf_op jit(solution)/shard_map/ppermute | solution.py:493
  115.6 44.3 %collective-permute-start.14 = (bf16[96,3584]{1,0:T(8,128)(2,1)S(1)}, bf16[96,3584]{1,0:T(8,128)(2,1)S(1)}, u32[]{:S(2)}, u32[]{:S(2)}) collective-permute-start(bf16[96,3584]{1,0:T(8,128)(2,1)S(1)} %get-tuple-element.41.refs_0_), channel_id=1, source_target_pairs={{0,2},{1,3},{2,0},{3,1},{4,6},{5,7},{6,4},{7,5},{8,10},{9,11},{10,... | collective-permute-start | bytes 2064392 | tf_op jit(solution)/shard_map/ppermute | solution.py:37
  117.1 45.3 %collective-permute-start.13 = (bf16[96,3584]{1,0:T(8,128)(2,1)S(1)}, bf16[96,3584]{1,0:T(8,128)(2,1)S(1)}, u32[]{:S(2)}, u32[]{:S(2)}) collective-permute-start(bf16[96,3584]{1,0:T(8,128)(2,1)S(1)} %get-tuple-element.41.refs_0_), channel_id=1, source_target_pairs={{0,1},{1,0},{2,3},{3,2},{4,5},{5,4},{6,7},{7,6},{8,9},{9,8},{10,11... | collective-permute-start | bytes 2064392 | tf_op jit(solution)/shard_map/ppermute | solution.py:37
  117.7 42.2 %collective-permute-start.29 = (bf16[48,3584]{1,0:T(8,128)(2,1)S(1)}, bf16[48,3584]{1,0:T(8,128)(2,1)S(1)}, u32[]{:S(2)}, u32[]{:S(2)}) collective-permute-start(bf16[48,3584]{1,0:T(8,128)(2,1)S(1)} %get-tuple-element.53), channel_id=1, source_target_pairs={{0,16},{4,20},{8,24},{12,28},{16,0},{20,4},{24,8},{28,12},{1,17},{... | collective-permute-start | bytes 1032200 | tf_op jit(solution)/shard_map/ppermute | solution.py:42
  165.1 20.8 %collective-permute-start.26 = (bf16[4,112,1792]{2,1,0:T(8,128)(2,1)}, bf16[4,112,1792]{2,1,0:T(8,128)(2,1)S(1)}, u32[]{:S(2)}, u32[]{:S(2)}) collective-permute-start(bf16[4,112,1792]{2,1,0:T(8,128)(2,1)} %get-tuple-element.77.refs_0_), channel_id=1, source_target_pairs={{0,4},{4,0},{8,12},{12,8},{16,20},{20,16},{24,28},{28,24},{1,5},{5... | collective-permute-start | bytes 4816904 | tf_op jit(solution)/shard_map/ppermute | solution.py:42
  183.3 39.1 %collective-permute-start.25 = (bf16[4,112,1792]{2,1,0:T(8,128)(2,1)}, bf16[4,112,1792]{2,1,0:T(8,128)(2,1)}, u32[]{:S(2)}, u32[]{:S(2)}) collective-permute-start(bf16[4,112,1792]{2,1,0:T(8,128)(2,1)} %collective-permute-done.23), channel_id=1, source_target_pairs={{8,0},{12,4},{9,1},{13,5},{10,2},{14,6},{11,3},{15,7}} | collective-permute-start | bytes 4816904 | tf_op jit(solution)/shard_map/ppermute | solution.py:493
  185.9 36.5 %collective-permute-start.28 = (bf16[4,112,1792]{2,1,0:T(8,128)(2,1)S(1)}, bf16[4,112,1792]{2,1,0:T(8,128)(2,1)}, u32[]{:S(2)}, u32[]{:S(2)}) collective-permute-start(bf16[4,112,1792]{2,1,0:T(8,128)(2,1)S(1)} %get-tuple-element.71.refs_0_), channel_id=1, source_target_pairs={{0,4},{4,0},{8,12},{12,8},{16,20},{20,16},{24,28},{28,24},{1,5},{5... | collective-permute-start | bytes 4816904 | tf_op jit(solution)/shard_map/ppermute | solution.py:42
  227.3 29.7 %collective-permute-start.15 = (bf16[96,3584]{1,0:T(8,128)(2,1)S(1)}, bf16[96,3584]{1,0:T(8,128)(2,1)}, u32[]{:S(2)}, u32[]{:S(2)}) collective-permute-start(bf16[96,3584]{1,0:T(8,128)(2,1)S(1)} %copy-done.16), channel_id=1, source_target_pairs={{0,3},{1,2},{2,1},{3,0},{4,7},{5,6},{6,5},{7,4},{8,11},{9,10},{10,... | collective-permute-start | bytes 2064392 | tf_op jit(solution)/shard_map/ppermute | solution.py:37
  241.2 24.6 %collective-permute-start.48 = (bf16[192,896]{1,0:T(8,128)(2,1)S(1)}, bf16[192,896]{1,0:T(8,128)(2,1)S(1)}, u32[]{:S(2)}, u32[]{:S(2)}) collective-permute-start(bf16[192,896]{1,0:T(8,128)(2,1)S(1)} %gate_up.5), channel_id=1, source_target_pairs={{0,16},{4,20},{8,24},{12,28},{16,0},{20,4},{24,8},{28,12},{1,17},{... | collective-permute-start | bytes 1032200 | tf_op jit(solution)/shard_map/ppermute | solution.py:42
  278.0 31.6 %collective-permute-start.43 = (bf16[48,3584]{1,0:T(8,128)(2,1)S(1)}, bf16[48,3584]{1,0:T(8,128)(2,1)S(1)}, u32[]{:S(2)}, u32[]{:S(2)}) collective-permute-start(bf16[48,3584]{1,0:T(8,128)(2,1)S(1)} %get-tuple-element.61), channel_id=1, source_target_pairs={{0,2},{1,3},{2,0},{3,1},{4,6},{5,7},{6,4},{7,5},{8,10},{9,11},{10,... | collective-permute-start | bytes 1032200 | tf_op jit(solution)/shard_map/ppermute | solution.py:37
  280.5 29.0 %collective-permute-start.44 = (bf16[48,3584]{1,0:T(8,128)(2,1)S(1)}, bf16[48,3584]{1,0:T(8,128)(2,1)S(1)}, u32[]{:S(2)}, u32[]{:S(2)}) collective-permute-start(bf16[48,3584]{1,0:T(8,128)(2,1)S(1)} %get-tuple-element.62), channel_id=1, source_target_pairs={{0,3},{1,2},{2,1},{3,0},{4,7},{5,6},{6,5},{7,4},{8,11},{9,10},{10,... | collective-permute-start | bytes 1032200 | tf_op jit(solution)/shard_map/ppermute | solution.py:37
  288.6 23.8 %collective-permute-start.54 = (bf16[48,3584]{1,0:T(8,128)(2,1)S(1)}, bf16[48,3584]{1,0:T(8,128)(2,1)S(1)}, u32[]{:S(2)}, u32[]{:S(2)}) collective-permute-start(bf16[48,3584]{1,0:T(8,128)(2,1)S(1)} %out_norm.3.refs_0_), channel_id=1, source_target_pairs={{0,3},{1,2},{2,1},{3,0},{4,7},{5,6},{6,5},{7,4},{8,11},{9,10},{10,... | collective-permute-start | bytes 1032200 | tf_op jit(solution)/shard_map/ppermute | solution.py:37
  290.1 34.2 %collective-permute-start.53 = (bf16[48,3584]{1,0:T(8,128)(2,1)S(1)}, bf16[48,3584]{1,0:T(8,128)(2,1)S(1)}, u32[]{:S(2)}, u32[]{:S(2)}) collective-permute-start(bf16[48,3584]{1,0:T(8,128)(2,1)S(1)} %out_norm.3.refs_0_), channel_id=1, source_target_pairs={{0,2},{1,3},{2,0},{3,1},{4,6},{5,7},{6,4},{7,5},{8,10},{9,11},{10,... | collective-permute-start | bytes 1032200 | tf_op jit(solution)/shard_map/ppermute | solution.py:37
  295.3 28.9 %collective-permute-start.52 = (bf16[48,3584]{1,0:T(8,128)(2,1)S(1)}, bf16[48,3584]{1,0:T(8,128)(2,1)S(1)}, u32[]{:S(2)}, u32[]{:S(2)}) collective-permute-start(bf16[48,3584]{1,0:T(8,128)(2,1)S(1)} %out_norm.3.refs_0_), channel_id=1, source_target_pairs={{0,1},{1,0},{2,3},{3,2},{4,5},{5,4},{6,7},{7,6},{8,9},{9,8},{10,11... | collective-permute-start | bytes 1032200 | tf_op jit(solution)/shard_map/ppermute | solution.py:37
  311.5 20.1 %collective-permute-start.46 = (bf16[48,3584]{1,0:T(8,128)(2,1)S(1)}, bf16[48,3584]{1,0:T(8,128)(2,1)S(1)}, u32[]{:S(2)}, u32[]{:S(2)}) collective-permute-start(bf16[48,3584]{1,0:T(8,128)(2,1)S(1)} %out_norm.2.refs_0_), channel_id=1, source_target_pairs={{0,2},{1,3},{2,0},{3,1},{4,6},{5,7},{6,4},{7,5},{8,10},{9,11},{10,... | collective-permute-start | bytes 1032200 | tf_op jit(solution)/shard_map/ppermute | solution.py:37
  (87 other events, 740.0 us)
where the time goes:
time: 341 us; the launch traced here: 336 us
  waiting for transfers between devices  141 us (41%)
  starting transfers between devices  85.1 us (25%)
  Pallas kernels  54.2 us (16%)
  local copies, waits for them, and re-layouts  45.5 us (13%)
  other arithmetic  8.83 us (3%)
    ppermute x27, waiting for transfers between devices, tp_swap(): return lax.ppermute(values, 'tp', [(i, i ^ bits) for i in range(size)])  64.6 us
    ppermute x18, waiting for transfers between devices, seq_swap(): return lax.ppermute(values, 'seq', [(i, i ^ bits) for i in range(size)])  42.4 us
    unnamed x112, local copies, waits for them, and re-layouts  38.8 us
    ppermute x27, starting transfers between devices, tp_swap(): return lax.ppermute(values, 'tp', [(i, i ^ bits) for i in range(size)])  33.7 us
    ppermute x3, waiting for transfers between devices, down(): return lax.ppermute(values, 'seq', pairs)  22.9 us
    ppermute x4, starting transfers between devices, seq_up(): return lax.ppermute(values, 'seq', [(i, i + 2) for i in range(size - 2)])  18.5 us
    pallas_call x3, Pallas kernels, gate_up_act(): pl.pallas_call(functools.partial(gate_up_kernel, parts=parts, picked=pick...  17.3 us
    ppermute x18, starting transfers between devices, seq_swap(): return lax.ppermute(values, 'seq', [(i, i ^ bits) for i in range(size)])  14.6 us
  transfers between devices with their start and end apart: 55, of which 28 were waited for; matrix products, arithmetic and copies ran while one was open for 2% of the time, Pallas kernels for 15%

commit v1 on v0

--- a/solution.py
+++ b/solution.py
@@ -69,7 +69,7 @@
         fetches[-1].start()
     first = place_ref[1]
     stacked = PER_GROUP * rows
-    at = first + lax.rem(lax.broadcasted_iota(jnp.int32, (stacked, 1), 0), rows)
+    at = first + lax.rem(lax.broadcasted_iota(jnp.int32, (1, stacked), 1), rows)
     start = jnp.zeros_like(at)
     lowest = jnp.int32(0)
     for p in range(prompts):
@@ -85,45 +85,48 @@
                 for r in range(PER_GROUP)
             ],
             axis=0,
-        )
-
-        def scores_of(keys, base, queries=queries):
+        ) * jnp.bfloat16(HEAD_DIM ** (-0.5))
+
+        def scores_of(keys, base, own, queries=queries):
             scores = lax.dot_general(
-                queries, keys, (((1,), (1,)), ((), ())), preferred_element_type=jnp.float32
-            ) * (HEAD_DIM ** (-0.5))
-            places = base + lax.broadcasted_iota(jnp.int32, (1, rows), 1)
-            return jnp.where((places >= start) & (places <= at), scores, -1e30)
+                keys, queries, (((1,), (1,)), ((), ())), preferred_element_type=jnp.float32
+            )
+            places = base + lax.broadcasted_iota(jnp.int32, scores.shape, 0)
+            kept = (places >= start) & (places <= at) if own else places >= start
+            return jnp.where(kept, scores, -1e30)
+
+        def blend(values, weights):
+            return lax.dot_general(
+                values,
+                weights.astype(jnp.bfloat16),
+                (((0,), (0,)), ((), ())),
+                preferred_element_type=jnp.float32,
+            )
 
         own_keys = joined_ref[:, col + head_cols : col + head_cols + HEAD_DIM]
         own_values = joined_ref[:, col + head_cols + HEAD_DIM : col + GROUP_COLS]
-        scores = scores_of(own_keys, first)
-        top = jnp.max(scores, axis=1, keepdims=True)
+        scores = scores_of(own_keys, first, True)
+        top = jnp.max(scores, axis=0, keepdims=True)
         weights = jnp.exp(scores - top)
-        peak[...] = jnp.broadcast_to(top, peak.shape)
-        total[...] = jnp.broadcast_to(jnp.sum(weights, axis=1, keepdims=True), total.shape)
-        acc[...] = jnp.dot(
-            weights.astype(jnp.bfloat16), own_values, preferred_element_type=jnp.float32
-        )
+        peak[...] = top
+        total[...] = jnp.sum(weights, axis=0, keepdims=True)
+        acc[...] = blend(own_values, weights)
         for i in range(blocks):
             base = place_ref[2 + i]
             kv_ref = kv_refs[i * groups + g]
 
             @pl.when((base >= 0) & (base + rows > lowest) & (base < first))
-            def _(base=base, kv_ref=kv_ref, scores_of=scores_of):
-                scores = scores_of(kv_ref[:, :HEAD_DIM], base)
-                before = peak[:, :1]
-                top = jnp.maximum(before, jnp.max(scores, axis=1, keepdims=True))
+            def _(base=base, kv_ref=kv_ref, scores_of=scores_of, blend=blend):
+                scores = scores_of(kv_ref[:, :HEAD_DIM], base, False)
+                before = peak[...]
+                top = jnp.maximum(before, jnp.max(scores, axis=0, keepdims=True))
                 weights = jnp.exp(scores - top)
                 shrink = jnp.exp(before - top)
-                peak[...] = jnp.broadcast_to(top, peak.shape)
-                total[...] = total[...] * shrink + jnp.sum(weights, axis=1, keepdims=True)
-                acc[...] = acc[...] * shrink + jnp.dot(
-                    weights.astype(jnp.bfloat16),
-                    kv_ref[:, HEAD_DIM:],
-                    preferred_element_type=jnp.float32,
-                )
-
-        result = (acc[...] / total[:, :1]).astype(jnp.bfloat16)
+                peak[...] = top
+                total[...] = total[...] * shrink + jnp.sum(weights, axis=0, keepdims=True)
+                acc[...] = acc[...] * shrink + blend(kv_ref[:, HEAD_DIM:], weights)
+
+        result = (acc[...] / total[...]).T.astype(jnp.bfloat16)
         attended = jnp.concatenate(
             [result[r * rows : (r + 1) * rows] for r in range(PER_GROUP)], axis=1
         )
@@ -162,9 +165,9 @@
         + [pl.BlockSpec(memory_space=pltpu.VMEM)] * (count * groups),
         out_specs=[pl.BlockSpec(memory_space=pltpu.VMEM)] * (parts + 1),
         scratch_shapes=[
-            pltpu.VMEM((stacked, 128), jnp.float32),
-            pltpu.VMEM((stacked, 128), jnp.float32),
-            pltpu.VMEM((stacked, HEAD_DIM), jnp.float32),
+            pltpu.VMEM((1, stacked), jnp.float32),
+            pltpu.VMEM((1, stacked), jnp.float32),
+            pltpu.VMEM((HEAD_DIM, stacked), jnp.float32),
             pltpu.VMEM((rows, width), jnp.float32),
             pltpu.VMEM(o_weight.shape, jnp.bfloat16),
             pltpu.SemaphoreType.DMA((groups,)),

time: 341 us -> 325 us (0.953); the launches traced: 336 us -> 326 us
  waiting for transfers between devices: 141 us -> 131 us
    ppermute x27, waiting for transfers between devices: 64.6 us -> 61 us  [tp_swap(): return lax.ppermute(values, 'tp', [(i, i ^ bits) for i in range(size)])]
    ppermute x3, waiting for transfers between devices: 22.9 us -> 19.4 us  [down(): return lax.ppermute(values, 'seq', pairs)]
  transfers between devices with their start and end apart: 55 -> 55, of which waited for: 28 -> 30; matrix products, arithmetic and copies ran while one was open for 2% -> 2% of each run, Pallas kernels for 15% -> 16%
where the time goes in v1:
time: 325 us; the launch traced here: 326 us
  waiting for transfers between devices  131 us (40%)
  starting transfers between devices  85.7 us (26%)
  Pallas kernels  54.3 us (17%)
  local copies, waits for them, and re-layouts  45.2 us (14%)
  other arithmetic  8.83 us (3%)
    ppermute x27, waiting for transfers between devices, tp_swap(): return lax.ppermute(values, 'tp', [(i, i ^ bits) for i in range(size)])  61 us
    ppermute x18, waiting for transfers between devices, seq_swap(): return lax.ppermute(values, 'seq', [(i, i ^ bits) for i in range(size)])  39.2 us
    unnamed x112, local copies, waits for them, and re-layouts  38.6 us
    ppermute x27, starting transfers between devices, tp_swap(): return lax.ppermute(values, 'tp', [(i, i ^ bits) for i in range(size)])  32.7 us
    ppermute x3, waiting for transfers between devices, down(): return lax.ppermute(values, 'seq', pairs)  19.4 us
    ppermute x4, starting transfers between devices, seq_up(): return lax.ppermute(values, 'seq', [(i, i + 2) for i in range(size - 2)])  18.5 us
    pallas_call x3, Pallas kernels, gate_up_act(): pl.pallas_call(functools.partial(gate_up_kernel, parts=parts, picked=pick...  17.3 us
    ppermute x18, starting transfers between devices, seq_swap(): return lax.ppermute(values, 'seq', [(i, i ^ bits) for i in range(size)])  16.2 us
  transfers between devices with their start and end apart: 55, of which 30 were waited for; matrix products, arithmetic and copies ran while one was open for 2% of the time, Pallas kernels for 16%

profile of v1, /device:TPU:0, one launch (start us, length us, event | category | flops | bytes accessed | tf_op | source)
XLA Modules:
  0.0 325.7 jit_solution(1158449068059076837)
XLA Ops:
  4.7 4.0 %collective-permute-start.18 = (bf16[2,112,1792]{2,1,0:T(8,128)(2,1)S(1)}, bf16[2,112,1792]{2,1,0:T(8,128)(2,1)S(1)}, u32[]{:S(2)}, u32[]{:S(2)}) collective-permute-start(bf16[2,112,1792]{2,1,0:T(8,128)(2,1)S(1)} %get-tuple-element.67), channel_id=1, source_target_pairs={{0,3},{1,2},{2,1},{3,0},{4,7},{5,6},{6,5},{7,4},{8,11},{9,10},{10,... | collective-permute-start | bytes 2408456 | tf_op jit(solution)/shard_map/ppermute | solution.py:37
  9.3 3.9 %collective-permute-start.3 = (bf16[384,512]{1,0:T(8,128)(2,1)S(1)}, bf16[384,512]{1,0:T(8,128)(2,1)S(1)}, u32[]{:S(2)}, u32[]{:S(2)}) collective-permute-start(bf16[384,512]{1,0:T(8,128)(2,1)S(1)} %get-tuple-element.80), channel_id=1, source_target_pairs={{0,8},{4,12},{8,16},{12,20},{16,24},{20,28},{1,9},{5,13},{9,17},{1... | collective-permute-start | bytes 1179656 | tf_op jit(solution)/shard_map/ppermute | solution.py:47
  13.2 4.3 %collective-permute-start.2 = (bf16[384,512]{1,0:T(8,128)(2,1)S(1)}, bf16[384,512]{1,0:T(8,128)(2,1)}, u32[]{:S(2)}, u32[]{:S(2)}) collective-permute-start(bf16[384,512]{1,0:T(8,128)(2,1)S(1)} %get-tuple-element.81), channel_id=1, source_target_pairs={{0,8},{4,12},{8,16},{12,20},{16,24},{20,28},{1,9},{5,13},{9,17},{1... | collective-permute-start | bytes 1179656 | tf_op jit(solution)/shard_map/ppermute | solution.py:47
  17.4 5.3 %collective-permute-done.3.refs_3_ = bf16[384,512]{1,0:T(8,128)(2,1)S(1)} collective-permute-done((bf16[384,512]{1,0:T(8,128)(2,1)S(1)}, bf16[384,512]{1,0:T(8,128)(2,1)S(1)}, u32[]{:S(2)}, u32[]{:S(2)}) %collective-permute-start.3) | collective-permute-done | bytes 393248 | tf_op jit(solution)/shard_map/ppermute | solution.py:47
  22.7 5.2 %collective-permute-start.7 = (bf16[384,512]{1,0:T(8,128)(2,1)S(1)}, bf16[384,512]{1,0:T(8,128)(2,1)}, u32[]{:S(2)}, u32[]{:S(2)}) collective-permute-start(bf16[384,512]{1,0:T(8,128)(2,1)S(1)} %collective-permute-done.3.refs_3_), channel_id=1, source_target_pairs={{0,8},{4,12},{8,16},{12,20},{16,24},{20,28},{1,9},{5,13},{9,17},{1... | collective-permute-start | bytes 1179656 | tf_op jit(solution)/shard_map/ppermute | solution.py:47
  31.1 5.2 %collective-permute-start.6 = (bf16[384,512]{1,0:T(8,128)(2,1)}, bf16[384,512]{1,0:T(8,128)(2,1)}, u32[]{:S(2)}, u32[]{:S(2)}) collective-permute-start(bf16[384,512]{1,0:T(8,128)(2,1)} %collective-permute-done.2.refs_2_), channel_id=1, source_target_pairs={{0,8},{4,12},{8,16},{12,20},{16,24},{20,28},{1,9},{5,13},{9,17},{1... | collective-permute-start | bytes 1179656 | tf_op jit(solution)/shard_map/ppermute | solution.py:47
  36.4 7.4 %collective-permute-done.17.refs_2_ = bf16[2,112,1792]{2,1,0:T(8,128)(2,1)S(1)} collective-permute-done((bf16[2,112,1792]{2,1,0:T(8,128)(2,1)S(1)}, bf16[2,112,1792]{2,1,0:T(8,128)(2,1)S(1)}, u32[]{:S(2)}, u32[]{:S(2)}) %collective-permute-start.17) | collective-permute-done | bytes 802848 | tf_op jit(solution)/shard_map/ppermute | solution.py:37
  47.3 6.2 %collective-permute-start.19 = (bf16[4,112,1792]{2,1,0:T(8,128)(2,1)S(1)}, bf16[4,112,1792]{2,1,0:T(8,128)(2,1)}, u32[]{:S(2)}, u32[]{:S(2)}) collective-permute-start(bf16[4,112,1792]{2,1,0:T(8,128)(2,1)S(1)} %get-tuple-element.46), channel_id=1, source_target_pairs={{0,8},{4,12},{8,16},{12,20},{16,24},{20,28},{1,9},{5,13},{9,17},{1... | collective-permute-start | bytes 4816904 | tf_op jit(solution)/shard_map/ppermute | solution.py:492
  64.1 9.5 %attention.1 = (bf16[96,3584]{1,0:T(8,128)(2,1)S(1)}, bf16[96,3584]{1,0:T(8,128)(2,1)S(1)}, bf16[96,3584]{1,0:T(8,128)(2,1)S(1)}, bf16[96,3584]{1,0:T(8,128)(2,1)}, bf16[16,128]{1,0:T(8,128)(2,1)S(1)}) custom-call(s32[4]{0:T(128)S(1)} %bitcast.45, s32[7]{0:T(128)S(1)} %stack.130.place_ref, bf16[384,2048]{1,0:T(8,128)(2,1)} %joined_ref.1, ...), custom_call_target="tpu_custom_call" | custom-call | flops 2000000000 | bytes 1000 | tf_op jit(solution)/shard_map/attention/pallas_call | solution.py:159
  88.7 6.1 %collective-permute-start.22 = (bf16[4,112,1792]{2,1,0:T(8,128)(2,1)}, bf16[4,112,1792]{2,1,0:T(8,128)(2,1)}, u32[]{:S(2)}, u32[]{:S(2)}) collective-permute-start(bf16[4,112,1792]{2,1,0:T(8,128)(2,1)} %get-tuple-element.78), channel_id=1, source_target_pairs={{0,8},{4,12},{8,16},{12,20},{16,24},{20,28},{1,9},{5,13},{9,17},{1... | collective-permute-start | bytes 4816904 | tf_op jit(solution)/shard_map/ppermute | solution.py:492
  96.3 15.0 %collective-permute-done.11.refs_2_ = bf16[96,3584]{1,0:T(8,128)(2,1)S(1)} collective-permute-done((bf16[96,3584]{1,0:T(8,128)(2,1)}, bf16[96,3584]{1,0:T(8,128)(2,1)S(1)}, u32[]{:S(2)}, u32[]{:S(2)}) %collective-permute-start.11) | collective-permute-done | bytes 688160 | tf_op jit(solution)/shard_map/ppermute | solution.py:37
  116.3 9.4 %collective-permute-start.29 = (bf16[48,3584]{1,0:T(8,128)(2,1)S(1)}, bf16[48,3584]{1,0:T(8,128)(2,1)S(1)}, u32[]{:S(2)}, u32[]{:S(2)}) collective-permute-start(bf16[48,3584]{1,0:T(8,128)(2,1)S(1)} %get-tuple-element.53), channel_id=1, source_target_pairs={{0,16},{4,20},{8,24},{12,28},{16,0},{20,4},{24,8},{28,12},{1,17},{... | collective-permute-start | bytes 1032200 | tf_op jit(solution)/shard_map/ppermute | solution.py:42
  125.6 32.9 %collective-permute-done.29.mark_ref.refs_0_ = bf16[48,3584]{1,0:T(8,128)(2,1)S(1)} collective-permute-done((bf16[48,3584]{1,0:T(8,128)(2,1)S(1)}, bf16[48,3584]{1,0:T(8,128)(2,1)S(1)}, u32[]{:S(2)}, u32[]{:S(2)}) %collective-permute-start.29) | collective-permute-done | bytes 344096 | tf_op jit(solution)/shard_map/ppermute | solution.py:42
  195.9 16.9 %collective-permute-done.25 = bf16[4,112,1792]{2,1,0:T(8,128)(2,1)} collective-permute-done((bf16[4,112,1792]{2,1,0:T(8,128)(2,1)}, bf16[4,112,1792]{2,1,0:T(8,128)(2,1)}, u32[]{:S(2)}, u32[]{:S(2)}) %collective-permute-start.25) | collective-permute-done | bytes 1605664 | tf_op jit(solution)/shard_map/ppermute | solution.py:496
  227.2 4.1 %gate_up.5 = bf16[192,896]{1,0:T(8,128)(2,1)S(1)} custom-call(s32[1]{0:T(128)} %bitcast.9.half_ref, bf16[48,3584]{1,0:T(8,128)(2,1)S(1)} %collective-permute-done.29.mark_ref.refs_0_, bf16[48,3584]{1,0:T(8,128)(2,1)S(1)} %copy-done.34, bf16[48,3584]{1,0:T(8,128)(2,1)S(1)} %copy-done.32, bf16[48,3584]{1,0:T(8,128)(2,1)S(1)} %copy-done.30, ...), custom_call_target="tpu_custom_call" | custom-call | flops 1 | bytes 1000 | tf_op jit(solution)/shard_map/gate_up/pallas_call | solution.py:425
  231.3 4.6 %copy-done.6 = bf16[1792,3584]{1,0:T(8,128)(2,1)S(1)} copy-done((bf16[1792,3584]{1,0:T(8,128)(2,1)S(1)}, bf16[1792,3584]{1,0:T(8,128)(2,1)}, u32[]{:S(2)}) %copy-start.6) | copy-done | bytes 12845080
  238.8 5.3 %gate_up.4 = bf16[192,896]{1,0:T(8,128)(2,1)S(1)} custom-call(s32[1]{0:T(128)} %bitcast.9.half_ref, bf16[48,3584]{1,0:T(8,128)(2,1)} %collective-permute-done.33.refs_0_, bf16[48,3584]{1,0:T(8,128)(2,1)} %collective-permute-done.34.refs_1_, bf16[48,3584]{1,0:T(8,128)(2,1)} %collective-permute-done.35.refs_2_, bf16[48,3584]{1,0:T(8,128)(2,1)S(1)} %copy-done.36, ...), custom_call_target="tpu_custom_call" | custom-call | flops 1 | bytes 1000 | tf_op jit(solution)/shard_map/gate_up/pallas_call | solution.py:425
  247.1 7.9 %gate_up.3.own_ref.mark_ref = bf16[384,896]{1,0:T(8,128)(2,1)S(1)} custom-call(s32[1]{0:T(128)} %bitcast.9.half_ref, bf16[96,3584]{1,0:T(8,128)(2,1)S(1)} %copy-done.16, bf16[96,3584]{1,0:T(8,128)(2,1)S(1)} %copy-done.20, bf16[96,3584]{1,0:T(8,128)(2,1)S(1)} %copy-done.18, bf16[96,3584]{1,0:T(8,128)(2,1)} %collective-permute-done.15.refs_3_, ...), custom_call_target="tpu_custom_call" | custom-call | flops 1 | bytes 1000 | tf_op jit(solution)/shard_map/gate_up/pallas_call | solution.py:425
  263.5 4.0 %down.2 = (bf16[48,3584]{1,0:T(8,128)(2,1)S(1)}, bf16[48,3584]{1,0:T(8,128)(2,1)S(1)}, bf16[48,3584]{1,0:T(8,128)(2,1)S(1)}, bf16[48,3584]{1,0:T(8,128)(2,1)S(1)}) custom-call(s32[1]{0:T(128)} %bitcast.9.half_ref, bf16[384,896]{1,0:T(8,128)(2,1)S(1)} %gate_up.3.own_ref.mark_ref, bf16[192,896]{1,0:T(8,128)(2,1)S(1)} %collective-permute-done.41.returned_ref, ...), custom_call_target="tpu_custom_call" | custom-call | flops 1 | bytes 1000 | tf_op jit(solution)/shard_map/down/pallas_call | solution.py:298
  271.9 5.8 %collective-permute-done.50.refs_2_ = bf16[48,3584]{1,0:T(8,128)(2,1)S(1)} collective-permute-done((bf16[48,3584]{1,0:T(8,128)(2,1)S(1)}, bf16[48,3584]{1,0:T(8,128)(2,1)S(1)}, u32[]{:S(2)}, u32[]{:S(2)}) %collective-permute-start.50) | collective-permute-done | bytes 344096 | tf_op jit(solution)/shard_map/ppermute | solution.py:37
  281.6 4.1 %collective-permute-done.42.refs_1_ = bf16[48,3584]{1,0:T(8,128)(2,1)S(1)} collective-permute-done((bf16[48,3584]{1,0:T(8,128)(2,1)S(1)}, bf16[48,3584]{1,0:T(8,128)(2,1)S(1)}, u32[]{:S(2)}, u32[]{:S(2)}) %collective-permute-start.42) | collective-permute-done | bytes 344096 | tf_op jit(solution)/shard_map/ppermute | solution.py:37
  286.2 13.6 %collective-permute-done.43.refs_2_ = bf16[48,3584]{1,0:T(8,128)(2,1)S(1)} collective-permute-done((bf16[48,3584]{1,0:T(8,128)(2,1)S(1)}, bf16[48,3584]{1,0:T(8,128)(2,1)S(1)}, u32[]{:S(2)}, u32[]{:S(2)}) %collective-permute-start.43) | collective-permute-done | bytes 344096 | tf_op jit(solution)/shard_map/ppermute | solution.py:37
  303.8 5.2 %copy-done.3 = bf16[3584,2048]{1,0:T(8,128)(2,1)S(1)} copy-done((bf16[3584,2048]{1,0:T(8,128)(2,1)S(1)}, bf16[3584,2048]{1,0:T(8,128)(2,1)}, u32[]{:S(2)}) %copy-start.3) | copy-done | bytes 14680088
  310.0 4.5 %collective-permute-done.53.refs_2_ = bf16[48,3584]{1,0:T(8,128)(2,1)S(1)} collective-permute-done((bf16[48,3584]{1,0:T(8,128)(2,1)S(1)}, bf16[48,3584]{1,0:T(8,128)(2,1)S(1)}, u32[]{:S(2)}, u32[]{:S(2)}) %collective-permute-start.53) | collective-permute-done | bytes 344096 | tf_op jit(solution)/shard_map/ppermute | solution.py:37
  (229 shorter events, 134.8 us)
Async XLA Ops:
  4.7 31.7 %collective-permute-start.18 = (bf16[2,112,1792]{2,1,0:T(8,128)(2,1)S(1)}, bf16[2,112,1792]{2,1,0:T(8,128)(2,1)S(1)}, u32[]{:S(2)}, u32[]{:S(2)}) collective-permute-start(bf16[2,112,1792]{2,1,0:T(8,128)(2,1)S(1)} %get-tuple-element.67), channel_id=1, source_target_pairs={{0,3},{1,2},{2,1},{3,0},{4,7},{5,6},{6,5},{7,4},{8,11},{9,10},{10,... | collective-permute-start | bytes 2408456 | tf_op jit(solution)/shard_map/ppermute | solution.py:37
  8.6 35.1 %collective-permute-start.17 = (bf16[2,112,1792]{2,1,0:T(8,128)(2,1)S(1)}, bf16[2,112,1792]{2,1,0:T(8,128)(2,1)S(1)}, u32[]{:S(2)}, u32[]{:S(2)}) collective-permute-start(bf16[2,112,1792]{2,1,0:T(8,128)(2,1)S(1)} %get-tuple-element.68), channel_id=1, source_target_pairs={{0,2},{1,3},{2,0},{3,1},{4,6},{5,7},{6,4},{7,5},{8,10},{9,11},{10,... | collective-permute-start | bytes 2408456 | tf_op jit(solution)/shard_map/ppermute | solution.py:37
  9.1 34.9 %collective-permute-start.16 = (bf16[2,112,1792]{2,1,0:T(8,128)(2,1)S(1)}, bf16[2,112,1792]{2,1,0:T(8,128)(2,1)S(1)}, u32[]{:S(2)}, u32[]{:S(2)}) collective-permute-start(bf16[2,112,1792]{2,1,0:T(8,128)(2,1)S(1)} %get-tuple-element.69), channel_id=1, source_target_pairs={{0,1},{1,0},{2,3},{3,2},{4,5},{5,4},{6,7},{7,6},{8,9},{9,8},{10,11... | collective-permute-start | bytes 2408456 | tf_op jit(solution)/shard_map/ppermute | solution.py:37
  22.7 21.6 %collective-permute-start.7 = (bf16[384,512]{1,0:T(8,128)(2,1)S(1)}, bf16[384,512]{1,0:T(8,128)(2,1)}, u32[]{:S(2)}, u32[]{:S(2)}) collective-permute-start(bf16[384,512]{1,0:T(8,128)(2,1)S(1)} %collective-permute-done.3.refs_3_), channel_id=1, source_target_pairs={{0,8},{4,12},{8,16},{12,20},{16,24},{20,28},{1,9},{5,13},{9,17},{1... | collective-permute-start | bytes 1179656 | tf_op jit(solution)/shard_map/ppermute | solution.py:47
  46.0 37.8 %collective-permute-start.20 = (bf16[4,112,1792]{2,1,0:T(8,128)(2,1)S(1)}, bf16[4,112,1792]{2,1,0:T(8,128)(2,1)}, u32[]{:S(2)}, u32[]{:S(2)}) collective-permute-start(bf16[4,112,1792]{2,1,0:T(8,128)(2,1)S(1)} %get-tuple-element.45), channel_id=1, source_target_pairs={{8,0},{12,4},{16,8},{20,12},{24,16},{28,20},{9,1},{13,5},{17,9},{2... | collective-permute-start | bytes 4816904 | tf_op jit(solution)/shard_map/ppermute | solution.py:496
  47.3 37.6 %collective-permute-start.19 = (bf16[4,112,1792]{2,1,0:T(8,128)(2,1)S(1)}, bf16[4,112,1792]{2,1,0:T(8,128)(2,1)}, u32[]{:S(2)}, u32[]{:S(2)}) collective-permute-start(bf16[4,112,1792]{2,1,0:T(8,128)(2,1)S(1)} %get-tuple-element.46), channel_id=1, source_target_pairs={{0,8},{4,12},{8,16},{12,20},{16,24},{20,28},{1,9},{5,13},{9,17},{1... | collective-permute-start | bytes 4816904 | tf_op jit(solution)/shard_map/ppermute | solution.py:492
  79.3 32.0 %collective-permute-start.11 = (bf16[96,3584]{1,0:T(8,128)(2,1)}, bf16[96,3584]{1,0:T(8,128)(2,1)S(1)}, u32[]{:S(2)}, u32[]{:S(2)}) collective-permute-start(bf16[96,3584]{1,0:T(8,128)(2,1)} %copy-done.43), channel_id=1, source_target_pairs={{0,2},{1,3},{2,0},{3,1},{4,6},{5,7},{6,4},{7,5},{8,10},{9,11},{10,... | collective-permute-start | bytes 2064392 | tf_op jit(solution)/shard_map/ppermute | solution.py:37
  80.8 30.5 %collective-permute-start.12 = (bf16[96,3584]{1,0:T(8,128)(2,1)}, bf16[96,3584]{1,0:T(8,128)(2,1)S(1)}, u32[]{:S(2)}, u32[]{:S(2)}) collective-permute-start(bf16[96,3584]{1,0:T(8,128)(2,1)} %get-tuple-element.39), channel_id=1, source_target_pairs={{0,3},{1,2},{2,1},{3,0},{4,7},{5,6},{6,5},{7,4},{8,11},{9,10},{10,... | collective-permute-start | bytes 2064392 | tf_op jit(solution)/shard_map/ppermute | solution.py:37
  88.7 74.3 %collective-permute-start.22 = (bf16[4,112,1792]{2,1,0:T(8,128)(2,1)}, bf16[4,112,1792]{2,1,0:T(8,128)(2,1)}, u32[]{:S(2)}, u32[]{:S(2)}) collective-permute-start(bf16[4,112,1792]{2,1,0:T(8,128)(2,1)} %get-tuple-element.78), channel_id=1, source_target_pairs={{0,8},{4,12},{8,16},{12,20},{16,24},{20,28},{1,9},{5,13},{9,17},{1... | collective-permute-start | bytes 4816904 | tf_op jit(solution)/shard_map/ppermute | solution.py:492
  94.8 68.9 %collective-permute-start.23 = (bf16[4,112,1792]{2,1,0:T(8,128)(2,1)}, bf16[4,112,1792]{2,1,0:T(8,128)(2,1)}, u32[]{:S(2)}, u32[]{:S(2)}) collective-permute-start(bf16[4,112,1792]{2,1,0:T(8,128)(2,1)} %get-tuple-element.79), channel_id=1, source_target_pairs={{8,0},{12,4},{16,8},{20,12},{24,16},{28,20},{9,1},{13,5},{17,9},{2... | collective-permute-start | bytes 4816904 | tf_op jit(solution)/shard_map/ppermute | solution.py:496
  114.2 44.3 %collective-permute-start.14 = (bf16[96,3584]{1,0:T(8,128)(2,1)S(1)}, bf16[96,3584]{1,0:T(8,128)(2,1)S(1)}, u32[]{:S(2)}, u32[]{:S(2)}) collective-permute-start(bf16[96,3584]{1,0:T(8,128)(2,1)S(1)} %get-tuple-element.41.refs_0_), channel_id=1, source_target_pairs={{0,2},{1,3},{2,0},{3,1},{4,6},{5,7},{6,4},{7,5},{8,10},{9,11},{10,... | collective-permute-start | bytes 2064392 | tf_op jit(solution)/shard_map/ppermute | solution.py:37
  115.7 45.9 %collective-permute-start.13 = (bf16[96,3584]{1,0:T(8,128)(2,1)S(1)}, bf16[96,3584]{1,0:T(8,128)(2,1)S(1)}, u32[]{:S(2)}, u32[]{:S(2)}) collective-permute-start(bf16[96,3584]{1,0:T(8,128)(2,1)S(1)} %get-tuple-element.41.refs_0_), channel_id=1, source_target_pairs={{0,1},{1,0},{2,3},{3,2},{4,5},{5,4},{6,7},{7,6},{8,9},{9,8},{10,11... | collective-permute-start | bytes 2064392 | tf_op jit(solution)/shard_map/ppermute | solution.py:37
  116.3 42.2 %collective-permute-start.29 = (bf16[48,3584]{1,0:T(8,128)(2,1)S(1)}, bf16[48,3584]{1,0:T(8,128)(2,1)S(1)}, u32[]{:S(2)}, u32[]{:S(2)}) collective-permute-start(bf16[48,3584]{1,0:T(8,128)(2,1)S(1)} %get-tuple-element.53), channel_id=1, source_target_pairs={{0,16},{4,20},{8,24},{12,28},{16,0},{20,4},{24,8},{28,12},{1,17},{... | collective-permute-start | bytes 1032200 | tf_op jit(solution)/shard_map/ppermute | solution.py:42
  172.0 23.9 %collective-permute-start.24 = (bf16[4,112,1792]{2,1,0:T(8,128)(2,1)}, bf16[4,112,1792]{2,1,0:T(8,128)(2,1)}, u32[]{:S(2)}, u32[]{:S(2)}) collective-permute-start(bf16[4,112,1792]{2,1,0:T(8,128)(2,1)} %collective-permute-done.22), channel_id=1, source_target_pairs={{16,24},{20,28},{17,25},{21,29},{18,26},{22,30},{19,27},{23,31}} | collective-permute-start | bytes 4816904 | tf_op jit(solution)/shard_map/ppermute | solution.py:492
  174.5 38.2 %collective-permute-start.25 = (bf16[4,112,1792]{2,1,0:T(8,128)(2,1)}, bf16[4,112,1792]{2,1,0:T(8,128)(2,1)}, u32[]{:S(2)}, u32[]{:S(2)}) collective-permute-start(bf16[4,112,1792]{2,1,0:T(8,128)(2,1)} %collective-permute-done.23), channel_id=1, source_target_pairs={{8,0},{12,4},{9,1},{13,5},{10,2},{14,6},{11,3},{15,7}} | collective-permute-start | bytes 4816904 | tf_op jit(solution)/shard_map/ppermute | solution.py:496
  180.2 32.6 %collective-permute-start.28 = (bf16[4,112,1792]{2,1,0:T(8,128)(2,1)S(1)}, bf16[4,112,1792]{2,1,0:T(8,128)(2,1)}, u32[]{:S(2)}, u32[]{:S(2)}) collective-permute-start(bf16[4,112,1792]{2,1,0:T(8,128)(2,1)S(1)} %get-tuple-element.71.refs_0_), channel_id=1, source_target_pairs={{0,4},{4,0},{8,12},{12,8},{16,20},{20,16},{24,28},{28,24},{1,5},{5... | collective-permute-start | bytes 4816904 | tf_op jit(solution)/shard_map/ppermute | solution.py:42
  217.7 29.4 %collective-permute-start.15 = (bf16[96,3584]{1,0:T(8,128)(2,1)S(1)}, bf16[96,3584]{1,0:T(8,128)(2,1)}, u32[]{:S(2)}, u32[]{:S(2)}) collective-permute-start(bf16[96,3584]{1,0:T(8,128)(2,1)S(1)} %copy-done.16), channel_id=1, source_target_pairs={{0,3},{1,2},{2,1},{3,0},{4,7},{5,6},{6,5},{7,4},{8,11},{9,10},{10,... | collective-permute-start | bytes 2064392 | tf_op jit(solution)/shard_map/ppermute | solution.py:37
  231.2 24.9 %collective-permute-start.48 = (bf16[192,896]{1,0:T(8,128)(2,1)S(1)}, bf16[192,896]{1,0:T(8,128)(2,1)S(1)}, u32[]{:S(2)}, u32[]{:S(2)}) collective-permute-start(bf16[192,896]{1,0:T(8,128)(2,1)S(1)} %gate_up.5), channel_id=1, source_target_pairs={{0,16},{4,20},{8,24},{12,28},{16,0},{20,4},{24,8},{28,12},{1,17},{... | collective-permute-start | bytes 1032200 | tf_op jit(solution)/shard_map/ppermute | solution.py:42
  268.1 31.7 %collective-permute-start.43 = (bf16[48,3584]{1,0:T(8,128)(2,1)S(1)}, bf16[48,3584]{1,0:T(8,128)(2,1)S(1)}, u32[]{:S(2)}, u32[]{:S(2)}) collective-permute-start(bf16[48,3584]{1,0:T(8,128)(2,1)S(1)} %get-tuple-element.61), channel_id=1, source_target_pairs={{0,2},{1,3},{2,0},{3,1},{4,6},{5,7},{6,4},{7,5},{8,10},{9,11},{10,... | collective-permute-start | bytes 1032200 | tf_op jit(solution)/shard_map/ppermute | solution.py:37
  270.9 28.9 %collective-permute-start.44 = (bf16[48,3584]{1,0:T(8,128)(2,1)S(1)}, bf16[48,3584]{1,0:T(8,128)(2,1)S(1)}, u32[]{:S(2)}, u32[]{:S(2)}) collective-permute-start(bf16[48,3584]{1,0:T(8,128)(2,1)S(1)} %get-tuple-element.62), channel_id=1, source_target_pairs={{0,3},{1,2},{2,1},{3,0},{4,7},{5,6},{6,5},{7,4},{8,11},{9,10},{10,... | collective-permute-start | bytes 1032200 | tf_op jit(solution)/shard_map/ppermute | solution.py:37
  278.7 25.0 %collective-permute-start.54 = (bf16[48,3584]{1,0:T(8,128)(2,1)S(1)}, bf16[48,3584]{1,0:T(8,128)(2,1)S(1)}, u32[]{:S(2)}, u32[]{:S(2)}) collective-permute-start(bf16[48,3584]{1,0:T(8,128)(2,1)S(1)} %out_norm.3.refs_0_), channel_id=1, source_target_pairs={{0,3},{1,2},{2,1},{3,0},{4,7},{5,6},{6,5},{7,4},{8,11},{9,10},{10,... | collective-permute-start | bytes 1032200 | tf_op jit(solution)/shard_map/ppermute | solution.py:37
  280.2 34.2 %collective-permute-start.53 = (bf16[48,3584]{1,0:T(8,128)(2,1)S(1)}, bf16[48,3584]{1,0:T(8,128)(2,1)S(1)}, u32[]{:S(2)}, u32[]{:S(2)}) collective-permute-start(bf16[48,3584]{1,0:T(8,128)(2,1)S(1)} %out_norm.3.refs_0_), channel_id=1, source_target_pairs={{0,2},{1,3},{2,0},{3,1},{4,6},{5,7},{6,4},{7,5},{8,10},{9,11},{10,... | collective-permute-start | bytes 1032200 | tf_op jit(solution)/shard_map/ppermute | solution.py:37
  285.7 28.8 %collective-permute-start.52 = (bf16[48,3584]{1,0:T(8,128)(2,1)S(1)}, bf16[48,3584]{1,0:T(8,128)(2,1)S(1)}, u32[]{:S(2)}, u32[]{:S(2)}) collective-permute-start(bf16[48,3584]{1,0:T(8,128)(2,1)S(1)} %out_norm.3.refs_0_), channel_id=1, source_target_pairs={{0,1},{1,0},{2,3},{3,2},{4,5},{5,4},{6,7},{7,6},{8,9},{9,8},{10,11... | collective-permute-start | bytes 1032200 | tf_op jit(solution)/shard_map/ppermute | solution.py:37
  301.6 20.1 %collective-permute-start.46 = (bf16[48,3584]{1,0:T(8,128)(2,1)S(1)}, bf16[48,3584]{1,0:T(8,128)(2,1)S(1)}, u32[]{:S(2)}, u32[]{:S(2)}) collective-permute-start(bf16[48,3584]{1,0:T(8,128)(2,1)S(1)} %out_norm.2.refs_0_), channel_id=1, source_target_pairs={{0,2},{1,3},{2,0},{3,1},{4,6},{5,7},{6,4},{7,5},{8,10},{9,11},{10,... | collective-permute-start | bytes 1032200 | tf_op jit(solution)/shard_map/ppermute | solution.py:37
  (87 other events, 706.9 us)

commit v2 on v1

--- a/solution.py
+++ b/solution.py
@@ -637,13 +637,13 @@
         seq_swap(gate_up_act(pieces, [0], 1, packed, half), half_count)
         for pieces in partner_pieces
     ]
-    own_act = gate_up_act(own_pieces, list(range(chunks)), chunks, packed, half)
+    own_act = [gate_up_act(own_pieces, [c], chunks, packed, half) for c in range(chunks)]
     down_held = hold(down_weight, partner_pieces[0][0])
-    next_held = hold(next_weight, own_act)
+    next_held = hold(next_weight, own_act[0])
     result = None
     gathered = []
     for c in range(chunks):
-        ffw_out = down(own_act, returned[c], down_held, half, tp_count, c)
+        ffw_out = down(own_act[c], returned[c], down_held, half, tp_count, 0)
         next_in = out_norm(residual_mid, post_ffw_gain, next_gain, tp_scatter(ffw_out), c)
         gathered.append(tp_gather(next_in, tp_count))
     for c in range(chunks):

time: 325 us -> 330 us (1.015)
  local copies, waits for them, and re-layouts: 45.2 us -> 57.6 us
  starting transfers between devices: 85.7 us -> 79.6 us
  waiting for transfers between devices: 131 us -> 125 us
    unnamed x112 -> x114, local copies, waits for them, and re-layouts: 38.6 us -> 50.9 us
    ppermute x27, waiting for transfers between devices: 61 us -> 52.3 us  [tp_swap(): return lax.ppermute(values, 'tp', [(i, i ^ bits) for i in range(size)])]
    ppermute x18, starting transfers between devices: 16.2 us -> 10 us  [seq_swap(): return lax.ppermute(values, 'seq', [(i, i ^ bits) for i in range(size)])]
    pallas_call x3 -> x4, Pallas kernels: 17.3 us -> 19.9 us  [gate_up_act(): pl.pallas_call(functools.partial(gate_up_kernel, parts=parts, picked=pick...]
  transfers between devices with their start and end apart: 55 -> 55, of which waited for: 30 -> 26; matrix products, arithmetic and copies ran while one was open for 2% -> 2% of each run, Pallas kernels for 16% -> 16%
where the time goes in v2:
time: 330 us; the launch traced here: 329 us
  waiting for transfers between devices  125 us (38%)
  starting transfers between devices  79.6 us (24%)
  local copies, waits for them, and re-layouts  57.6 us (17%)
  Pallas kernels  57.2 us (17%)
  other arithmetic  8.83 us (3%)
    ppermute x27, waiting for transfers between devices, tp_swap(): return lax.ppermute(values, 'tp', [(i, i ^ bits) for i in range(size)])  52.3 us
    unnamed x114, local copies, waits for them, and re-layouts  50.9 us
    ppermute x18, waiting for transfers between devices, seq_swap(): return lax.ppermute(values, 'seq', [(i, i ^ bits) for i in range(size)])  41.6 us
    ppermute x27, starting transfers between devices, tp_swap(): return lax.ppermute(values, 'tp', [(i, i ^ bits) for i in range(size)])  33.1 us
    pallas_call x4, Pallas kernels, gate_up_act(): pl.pallas_call(functools.partial(gate_up_kernel, parts=parts, picked=pick...  19.9 us
    ppermute x3, waiting for transfers between devices, down(): return lax.ppermute(values, 'seq', pairs)  19.2 us
    ppermute x4, starting transfers between devices, seq_up(): return lax.ppermute(values, 'seq', [(i, i + 2) for i in range(size - 2)])  18.5 us
    ppermute x3, starting transfers between devices, up(): return lax.ppermute(values, 'seq', pairs)  14.1 us
  transfers between devices with their start and end apart: 55, of which 26 were waited for; matrix products, arithmetic and copies ran while one was open for 2% of the time, Pallas kernels for 16%

profile of v2, /device:TPU:0, one launch (start us, length us, event | category | flops | bytes accessed | tf_op | source)
XLA Modules:
  0.0 328.5 jit_solution(1990688910930331405)
XLA Ops:
  4.7 4.0 %collective-permute-start.18 = (bf16[2,112,1792]{2,1,0:T(8,128)(2,1)S(1)}, bf16[2,112,1792]{2,1,0:T(8,128)(2,1)S(1)}, u32[]{:S(2)}, u32[]{:S(2)}) collective-permute-start(bf16[2,112,1792]{2,1,0:T(8,128)(2,1)S(1)} %get-tuple-element.67), channel_id=1, source_target_pairs={{0,3},{1,2},{2,1},{3,0},{4,7},{5,6},{6,5},{7,4},{8,11},{9,10},{10,... | collective-permute-start | bytes 2408456 | tf_op jit(solution)/shard_map/ppermute | solution.py:37
  13.2 4.3 %collective-permute-start.2 = (bf16[384,512]{1,0:T(8,128)(2,1)S(1)}, bf16[384,512]{1,0:T(8,128)(2,1)}, u32[]{:S(2)}, u32[]{:S(2)}) collective-permute-start(bf16[384,512]{1,0:T(8,128)(2,1)S(1)} %get-tuple-element.81), channel_id=1, source_target_pairs={{0,8},{4,12},{8,16},{12,20},{16,24},{20,28},{1,9},{5,13},{9,17},{1... | collective-permute-start | bytes 1179656 | tf_op jit(solution)/shard_map/ppermute | solution.py:47
  17.4 5.3 %collective-permute-done.3.refs_3_ = bf16[384,512]{1,0:T(8,128)(2,1)S(1)} collective-permute-done((bf16[384,512]{1,0:T(8,128)(2,1)S(1)}, bf16[384,512]{1,0:T(8,128)(2,1)S(1)}, u32[]{:S(2)}, u32[]{:S(2)}) %collective-permute-start.3) | collective-permute-done | bytes 393248 | tf_op jit(solution)/shard_map/ppermute | solution.py:47
  22.7 5.1 %collective-permute-start.7 = (bf16[384,512]{1,0:T(8,128)(2,1)S(1)}, bf16[384,512]{1,0:T(8,128)(2,1)}, u32[]{:S(2)}, u32[]{:S(2)}) collective-permute-start(bf16[384,512]{1,0:T(8,128)(2,1)S(1)} %collective-permute-done.3.refs_3_), channel_id=1, source_target_pairs={{0,8},{4,12},{8,16},{12,20},{16,24},{20,28},{1,9},{5,13},{9,17},{1... | collective-permute-start | bytes 1179656 | tf_op jit(solution)/shard_map/ppermute | solution.py:47
  31.1 5.2 %collective-permute-start.6 = (bf16[384,512]{1,0:T(8,128)(2,1)}, bf16[384,512]{1,0:T(8,128)(2,1)}, u32[]{:S(2)}, u32[]{:S(2)}) collective-permute-start(bf16[384,512]{1,0:T(8,128)(2,1)} %collective-permute-done.2.refs_2_), channel_id=1, source_target_pairs={{0,8},{4,12},{8,16},{12,20},{16,24},{20,28},{1,9},{5,13},{9,17},{1... | collective-permute-start | bytes 1179656 | tf_op jit(solution)/shard_map/ppermute | solution.py:47
  36.4 7.4 %collective-permute-done.17.refs_2_ = bf16[2,112,1792]{2,1,0:T(8,128)(2,1)S(1)} collective-permute-done((bf16[2,112,1792]{2,1,0:T(8,128)(2,1)S(1)}, bf16[2,112,1792]{2,1,0:T(8,128)(2,1)S(1)}, u32[]{:S(2)}, u32[]{:S(2)}) %collective-permute-start.17) | collective-permute-done | bytes 802848 | tf_op jit(solution)/shard_map/ppermute | solution.py:37
  47.3 6.2 %collective-permute-start.19 = (bf16[4,112,1792]{2,1,0:T(8,128)(2,1)S(1)}, bf16[4,112,1792]{2,1,0:T(8,128)(2,1)}, u32[]{:S(2)}, u32[]{:S(2)}) collective-permute-start(bf16[4,112,1792]{2,1,0:T(8,128)(2,1)S(1)} %get-tuple-element.46), channel_id=1, source_target_pairs={{0,8},{4,12},{8,16},{12,20},{16,24},{20,28},{1,9},{5,13},{9,17},{1... | collective-permute-start | bytes 4816904 | tf_op jit(solution)/shard_map/ppermute | solution.py:492
  64.1 9.5 %attention.1 = (bf16[96,3584]{1,0:T(8,128)(2,1)S(1)}, bf16[96,3584]{1,0:T(8,128)(2,1)S(1)}, bf16[96,3584]{1,0:T(8,128)(2,1)S(1)}, bf16[96,3584]{1,0:T(8,128)(2,1)}, bf16[16,128]{1,0:T(8,128)(2,1)S(1)}) custom-call(s32[4]{0:T(128)S(1)} %bitcast.45, s32[7]{0:T(128)S(1)} %stack.130.place_ref, bf16[384,2048]{1,0:T(8,128)(2,1)} %joined_ref.1, ...), custom_call_target="tpu_custom_call" | custom-call | flops 2000000000 | bytes 1000 | tf_op jit(solution)/shard_map/attention/pallas_call | solution.py:159
  88.7 6.2 %collective-permute-start.22 = (bf16[4,112,1792]{2,1,0:T(8,128)(2,1)}, bf16[4,112,1792]{2,1,0:T(8,128)(2,1)}, u32[]{:S(2)}, u32[]{:S(2)}) collective-permute-start(bf16[4,112,1792]{2,1,0:T(8,128)(2,1)} %get-tuple-element.78), channel_id=1, source_target_pairs={{0,8},{4,12},{8,16},{12,20},{16,24},{20,28},{1,9},{5,13},{9,17},{1... | collective-permute-start | bytes 4816904 | tf_op jit(solution)/shard_map/ppermute | solution.py:492
  96.3 15.0 %collective-permute-done.11.refs_2_ = bf16[96,3584]{1,0:T(8,128)(2,1)S(1)} collective-permute-done((bf16[96,3584]{1,0:T(8,128)(2,1)}, bf16[96,3584]{1,0:T(8,128)(2,1)S(1)}, u32[]{:S(2)}, u32[]{:S(2)}) %collective-permute-start.11) | collective-permute-done | bytes 688160 | tf_op jit(solution)/shard_map/ppermute | solution.py:37
  119.4 36.1 %collective-permute-done.29.mark_ref.refs_0_ = bf16[48,3584]{1,0:T(8,128)(2,1)S(1)} collective-permute-done((bf16[48,3584]{1,0:T(8,128)(2,1)S(1)}, bf16[48,3584]{1,0:T(8,128)(2,1)S(1)}, u32[]{:S(2)}, u32[]{:S(2)}) %collective-permute-start.29) | collective-permute-done | bytes 344096 | tf_op jit(solution)/shard_map/ppermute | solution.py:42
  193.2 16.8 %collective-permute-done.25 = bf16[4,112,1792]{2,1,0:T(8,128)(2,1)} collective-permute-done((bf16[4,112,1792]{2,1,0:T(8,128)(2,1)}, bf16[4,112,1792]{2,1,0:T(8,128)(2,1)}, u32[]{:S(2)}, u32[]{:S(2)}) %collective-permute-start.25) | collective-permute-done | bytes 1605664 | tf_op jit(solution)/shard_map/ppermute | solution.py:496
  224.3 4.1 %gate_up.7 = bf16[192,896]{1,0:T(8,128)(2,1)S(1)} custom-call(s32[1]{0:T(128)} %bitcast.9.half_ref, bf16[48,3584]{1,0:T(8,128)(2,1)S(1)} %collective-permute-done.29.mark_ref.refs_0_, bf16[48,3584]{1,0:T(8,128)(2,1)S(1)} %copy-done.35, bf16[48,3584]{1,0:T(8,128)(2,1)S(1)} %copy-done.33, bf16[48,3584]{1,0:T(8,128)(2,1)S(1)} %copy-done.31, ...), custom_call_target="tpu_custom_call" | custom-call | flops 1 | bytes 1000 | tf_op jit(solution)/shard_map/gate_up/pallas_call | solution.py:425
  228.5 4.6 %copy-done.7 = bf16[1792,3584]{1,0:T(8,128)(2,1)S(1)} copy-done((bf16[1792,3584]{1,0:T(8,128)(2,1)S(1)}, bf16[1792,3584]{1,0:T(8,128)(2,1)}, u32[]{:S(2)}) %copy-start.7) | copy-done | bytes 12845080
  234.4 4.6 %copy-done.1 = bf16[1792,3584]{1,0:T(8,128)(2,1)} copy-done((bf16[1792,3584]{1,0:T(8,128)(2,1)}, bf16[1792,3584]{1,0:T(8,128)(2,1)S(1)}, u32[]{:S(2)}) %copy-start.1) | copy-done | bytes 12845080
  239.1 5.4 %gate_up.5 = bf16[192,896]{1,0:T(8,128)(2,1)S(1)} custom-call(s32[1]{0:T(128)} %bitcast.9.half_ref, bf16[48,3584]{1,0:T(8,128)(2,1)} %collective-permute-done.33.refs_0_, bf16[48,3584]{1,0:T(8,128)(2,1)} %collective-permute-done.34.refs_1_, bf16[48,3584]{1,0:T(8,128)(2,1)} %collective-permute-done.35.refs_2_, bf16[48,3584]{1,0:T(8,128)(2,1)S(1)} %copy-done.37, ...), custom_call_target="tpu_custom_call" | custom-call | flops 1 | bytes 1000 | tf_op jit(solution)/shard_map/gate_up/pallas_call | solution.py:425
  247.5 5.2 %gate_up.6.mark_ref.own_ref = bf16[192,896]{1,0:T(8,128)(2,1)S(1)} custom-call(s32[1]{0:T(128)} %bitcast.9.half_ref, bf16[96,3584]{1,0:T(8,128)(2,1)S(1)} %copy-done.13, bf16[96,3584]{1,0:T(8,128)(2,1)S(1)} %copy-done.17, bf16[96,3584]{1,0:T(8,128)(2,1)S(1)} %copy-done.15, bf16[96,3584]{1,0:T(8,128)(2,1)} %collective-permute-done.15.refs_3_, ...), custom_call_target="tpu_custom_call" | custom-call | flops 1 | bytes 1000 | tf_op jit(solution)/shard_map/gate_up/pallas_call | solution.py:425
  252.7 4.6 %copy-done.2 = bf16[1792,3584]{1,0:T(8,128)(2,1)S(1)} copy-done((bf16[1792,3584]{1,0:T(8,128)(2,1)S(1)}, bf16[1792,3584]{1,0:T(8,128)(2,1)}, u32[]{:S(2)}) %copy-start.2) | copy-done | bytes 12845080
  264.9 5.2 %gate_up.4.own_ref = bf16[192,896]{1,0:T(8,128)(2,1)S(1)} custom-call(s32[1]{0:T(128)} %bitcast.9.half_ref, bf16[96,3584]{1,0:T(8,128)(2,1)S(1)} %copy-done.13, bf16[96,3584]{1,0:T(8,128)(2,1)S(1)} %copy-done.17, bf16[96,3584]{1,0:T(8,128)(2,1)S(1)} %copy-done.15, bf16[96,3584]{1,0:T(8,128)(2,1)} %collective-permute-done.15.refs_3_, ...), custom_call_target="tpu_custom_call" | custom-call | flops 1 | bytes 1000 | tf_op jit(solution)/shard_map/gate_up/pallas_call | solution.py:425
  270.1 4.6 %copy-done.3 = bf16[1792,3584]{1,0:T(8,128)(2,1)S(1)} copy-done((bf16[1792,3584]{1,0:T(8,128)(2,1)S(1)}, bf16[1792,3584]{1,0:T(8,128)(2,1)}, u32[]{:S(2)}) %copy-start.3) | copy-done | bytes 12845080
  284.8 4.9 %collective-permute-done.42.refs_1_ = bf16[48,3584]{1,0:T(8,128)(2,1)S(1)} collective-permute-done((bf16[48,3584]{1,0:T(8,128)(2,1)S(1)}, bf16[48,3584]{1,0:T(8,128)(2,1)S(1)}, u32[]{:S(2)}, u32[]{:S(2)}) %collective-permute-start.42) | collective-permute-done | bytes 344096 | tf_op jit(solution)/shard_map/ppermute | solution.py:37
  290.2 14.7 %collective-permute-done.43.refs_2_ = bf16[48,3584]{1,0:T(8,128)(2,1)S(1)} collective-permute-done((bf16[48,3584]{1,0:T(8,128)(2,1)S(1)}, bf16[48,3584]{1,0:T(8,128)(2,1)S(1)}, u32[]{:S(2)}, u32[]{:S(2)}) %collective-permute-start.43) | collective-permute-done | bytes 344096 | tf_op jit(solution)/shard_map/ppermute | solution.py:37
  309.0 5.2 %copy-done.4 = bf16[3584,2048]{1,0:T(8,128)(2,1)S(1)} copy-done((bf16[3584,2048]{1,0:T(8,128)(2,1)S(1)}, bf16[3584,2048]{1,0:T(8,128)(2,1)}, u32[]{:S(2)}) %copy-start.4) | copy-done | bytes 14680088
  315.2 4.5 %collective-permute-done.53.refs_2_ = bf16[48,3584]{1,0:T(8,128)(2,1)S(1)} collective-permute-done((bf16[48,3584]{1,0:T(8,128)(2,1)S(1)}, bf16[48,3584]{1,0:T(8,128)(2,1)S(1)}, u32[]{:S(2)}, u32[]{:S(2)}) %collective-permute-start.53) | collective-permute-done | bytes 344096 | tf_op jit(solution)/shard_map/ppermute | solution.py:37
  (232 shorter events, 139.1 us)
Async XLA Ops:
  4.7 31.7 %collective-permute-start.18 = (bf16[2,112,1792]{2,1,0:T(8,128)(2,1)S(1)}, bf16[2,112,1792]{2,1,0:T(8,128)(2,1)S(1)}, u32[]{:S(2)}, u32[]{:S(2)}) collective-permute-start(bf16[2,112,1792]{2,1,0:T(8,128)(2,1)S(1)} %get-tuple-element.67), channel_id=1, source_target_pairs={{0,3},{1,2},{2,1},{3,0},{4,7},{5,6},{6,5},{7,4},{8,11},{9,10},{10,... | collective-permute-start | bytes 2408456 | tf_op jit(solution)/shard_map/ppermute | solution.py:37
  8.6 35.1 %collective-permute-start.17 = (bf16[2,112,1792]{2,1,0:T(8,128)(2,1)S(1)}, bf16[2,112,1792]{2,1,0:T(8,128)(2,1)S(1)}, u32[]{:S(2)}, u32[]{:S(2)}) collective-permute-start(bf16[2,112,1792]{2,1,0:T(8,128)(2,1)S(1)} %get-tuple-element.68), channel_id=1, source_target_pairs={{0,2},{1,3},{2,0},{3,1},{4,6},{5,7},{6,4},{7,5},{8,10},{9,11},{10,... | collective-permute-start | bytes 2408456 | tf_op jit(solution)/shard_map/ppermute | solution.py:37
  9.1 34.9 %collective-permute-start.16 = (bf16[2,112,1792]{2,1,0:T(8,128)(2,1)S(1)}, bf16[2,112,1792]{2,1,0:T(8,128)(2,1)S(1)}, u32[]{:S(2)}, u32[]{:S(2)}) collective-permute-start(bf16[2,112,1792]{2,1,0:T(8,128)(2,1)S(1)} %get-tuple-element.69), channel_id=1, source_target_pairs={{0,1},{1,0},{2,3},{3,2},{4,5},{5,4},{6,7},{7,6},{8,9},{9,8},{10,11... | collective-permute-start | bytes 2408456 | tf_op jit(solution)/shard_map/ppermute | solution.py:37
  22.7 21.6 %collective-permute-start.7 = (bf16[384,512]{1,0:T(8,128)(2,1)S(1)}, bf16[384,512]{1,0:T(8,128)(2,1)}, u32[]{:S(2)}, u32[]{:S(2)}) collective-permute-start(bf16[384,512]{1,0:T(8,128)(2,1)S(1)} %collective-permute-done.3.refs_3_), channel_id=1, source_target_pairs={{0,8},{4,12},{8,16},{12,20},{16,24},{20,28},{1,9},{5,13},{9,17},{1... | collective-permute-start | bytes 1179656 | tf_op jit(solution)/shard_map/ppermute | solution.py:47
  46.0 37.8 %collective-permute-start.20 = (bf16[4,112,1792]{2,1,0:T(8,128)(2,1)S(1)}, bf16[4,112,1792]{2,1,0:T(8,128)(2,1)}, u32[]{:S(2)}, u32[]{:S(2)}) collective-permute-start(bf16[4,112,1792]{2,1,0:T(8,128)(2,1)S(1)} %get-tuple-element.45), channel_id=1, source_target_pairs={{8,0},{12,4},{16,8},{20,12},{24,16},{28,20},{9,1},{13,5},{17,9},{2... | collective-permute-start | bytes 4816904 | tf_op jit(solution)/shard_map/ppermute | solution.py:496
  47.3 37.6 %collective-permute-start.19 = (bf16[4,112,1792]{2,1,0:T(8,128)(2,1)S(1)}, bf16[4,112,1792]{2,1,0:T(8,128)(2,1)}, u32[]{:S(2)}, u32[]{:S(2)}) collective-permute-start(bf16[4,112,1792]{2,1,0:T(8,128)(2,1)S(1)} %get-tuple-element.46), channel_id=1, source_target_pairs={{0,8},{4,12},{8,16},{12,20},{16,24},{20,28},{1,9},{5,13},{9,17},{1... | collective-permute-start | bytes 4816904 | tf_op jit(solution)/shard_map/ppermute | solution.py:492
  79.3 32.0 %collective-permute-start.11 = (bf16[96,3584]{1,0:T(8,128)(2,1)}, bf16[96,3584]{1,0:T(8,128)(2,1)S(1)}, u32[]{:S(2)}, u32[]{:S(2)}) collective-permute-start(bf16[96,3584]{1,0:T(8,128)(2,1)} %copy-done.44), channel_id=1, source_target_pairs={{0,2},{1,3},{2,0},{3,1},{4,6},{5,7},{6,4},{7,5},{8,10},{9,11},{10,... | collective-permute-start | bytes 2064392 | tf_op jit(solution)/shard_map/ppermute | solution.py:37
  80.8 30.5 %collective-permute-start.12 = (bf16[96,3584]{1,0:T(8,128)(2,1)}, bf16[96,3584]{1,0:T(8,128)(2,1)S(1)}, u32[]{:S(2)}, u32[]{:S(2)}) collective-permute-start(bf16[96,3584]{1,0:T(8,128)(2,1)} %get-tuple-element.39), channel_id=1, source_target_pairs={{0,3},{1,2},{2,1},{3,0},{4,7},{5,6},{6,5},{7,4},{8,11},{9,10},{10,... | collective-permute-start | bytes 2064392 | tf_op jit(solution)/shard_map/ppermute | solution.py:37
  88.7 71.5 %collective-permute-start.22 = (bf16[4,112,1792]{2,1,0:T(8,128)(2,1)}, bf16[4,112,1792]{2,1,0:T(8,128)(2,1)}, u32[]{:S(2)}, u32[]{:S(2)}) collective-permute-start(bf16[4,112,1792]{2,1,0:T(8,128)(2,1)} %get-tuple-element.78), channel_id=1, source_target_pairs={{0,8},{4,12},{8,16},{12,20},{16,24},{20,28},{1,9},{5,13},{9,17},{1... | collective-permute-start | bytes 4816904 | tf_op jit(solution)/shard_map/ppermute | solution.py:492
  94.8 65.9 %collective-permute-start.23 = (bf16[4,112,1792]{2,1,0:T(8,128)(2,1)}, bf16[4,112,1792]{2,1,0:T(8,128)(2,1)}, u32[]{:S(2)}, u32[]{:S(2)}) collective-permute-start(bf16[4,112,1792]{2,1,0:T(8,128)(2,1)} %get-tuple-element.79), channel_id=1, source_target_pairs={{8,0},{12,4},{16,8},{20,12},{24,16},{28,20},{9,1},{13,5},{17,9},{2... | collective-permute-start | bytes 4816904 | tf_op jit(solution)/shard_map/ppermute | solution.py:496
  114.2 41.3 %collective-permute-start.14 = (bf16[96,3584]{1,0:T(8,128)(2,1)S(1)}, bf16[96,3584]{1,0:T(8,128)(2,1)S(1)}, u32[]{:S(2)}, u32[]{:S(2)}) collective-permute-start(bf16[96,3584]{1,0:T(8,128)(2,1)S(1)} %get-tuple-element.41.refs_0_), channel_id=1, source_target_pairs={{0,2},{1,3},{2,0},{3,1},{4,6},{5,7},{6,4},{7,5},{8,10},{9,11},{10,... | collective-permute-start | bytes 2064392 | tf_op jit(solution)/shard_map/ppermute | solution.py:37
  115.7 43.1 %collective-permute-start.13 = (bf16[96,3584]{1,0:T(8,128)(2,1)S(1)}, bf16[96,3584]{1,0:T(8,128)(2,1)S(1)}, u32[]{:S(2)}, u32[]{:S(2)}) collective-permute-start(bf16[96,3584]{1,0:T(8,128)(2,1)S(1)} %get-tuple-element.41.refs_0_), channel_id=1, source_target_pairs={{0,1},{1,0},{2,3},{3,2},{4,5},{5,4},{6,7},{7,6},{8,9},{9,8},{10,11... | collective-permute-start | bytes 2064392 | tf_op jit(solution)/shard_map/ppermute | solution.py:37
  116.2 39.3 %collective-permute-start.29 = (bf16[48,3584]{1,0:T(8,128)(2,1)S(1)}, bf16[48,3584]{1,0:T(8,128)(2,1)S(1)}, u32[]{:S(2)}, u32[]{:S(2)}) collective-permute-start(bf16[48,3584]{1,0:T(8,128)(2,1)S(1)} %get-tuple-element.53), channel_id=1, source_target_pairs={{0,16},{4,20},{8,24},{12,28},{16,0},{20,4},{24,8},{28,12},{1,17},{... | collective-permute-start | bytes 1032200 | tf_op jit(solution)/shard_map/ppermute | solution.py:42
  168.9 24.3 %collective-permute-start.24 = (bf16[4,112,1792]{2,1,0:T(8,128)(2,1)}, bf16[4,112,1792]{2,1,0:T(8,128)(2,1)}, u32[]{:S(2)}, u32[]{:S(2)}) collective-permute-start(bf16[4,112,1792]{2,1,0:T(8,128)(2,1)} %collective-permute-done.22), channel_id=1, source_target_pairs={{16,24},{20,28},{17,25},{21,29},{18,26},{22,30},{19,27},{23,31}} | collective-permute-start | bytes 4816904 | tf_op jit(solution)/shard_map/ppermute | solution.py:492
  171.5 38.5 %collective-permute-start.25 = (bf16[4,112,1792]{2,1,0:T(8,128)(2,1)}, bf16[4,112,1792]{2,1,0:T(8,128)(2,1)}, u32[]{:S(2)}, u32[]{:S(2)}) collective-permute-start(bf16[4,112,1792]{2,1,0:T(8,128)(2,1)} %collective-permute-done.23), channel_id=1, source_target_pairs={{8,0},{12,4},{9,1},{13,5},{10,2},{14,6},{11,3},{15,7}} | collective-permute-start | bytes 4816904 | tf_op jit(solution)/shard_map/ppermute | solution.py:496
  177.1 32.9 %collective-permute-start.28 = (bf16[4,112,1792]{2,1,0:T(8,128)(2,1)S(1)}, bf16[4,112,1792]{2,1,0:T(8,128)(2,1)}, u32[]{:S(2)}, u32[]{:S(2)}) collective-permute-start(bf16[4,112,1792]{2,1,0:T(8,128)(2,1)S(1)} %get-tuple-element.71.refs_0_), channel_id=1, source_target_pairs={{0,4},{4,0},{8,12},{12,8},{16,20},{20,16},{24,28},{28,24},{1,5},{5... | collective-permute-start | bytes 4816904 | tf_op jit(solution)/shard_map/ppermute | solution.py:42
  214.8 32.6 %collective-permute-start.15 = (bf16[96,3584]{1,0:T(8,128)(2,1)S(1)}, bf16[96,3584]{1,0:T(8,128)(2,1)}, u32[]{:S(2)}, u32[]{:S(2)}) collective-permute-start(bf16[96,3584]{1,0:T(8,128)(2,1)S(1)} %copy-done.13), channel_id=1, source_target_pairs={{0,3},{1,2},{2,1},{3,0},{4,7},{5,6},{6,5},{7,4},{8,11},{9,10},{10,... | collective-permute-start | bytes 2064392 | tf_op jit(solution)/shard_map/ppermute | solution.py:37
  228.4 24.2 %collective-permute-start.48 = (bf16[192,896]{1,0:T(8,128)(2,1)S(1)}, bf16[192,896]{1,0:T(8,128)(2,1)S(1)}, u32[]{:S(2)}, u32[]{:S(2)}) collective-permute-start(bf16[192,896]{1,0:T(8,128)(2,1)S(1)} %gate_up.7), channel_id=1, source_target_pairs={{0,16},{4,20},{8,24},{12,28},{16,0},{20,4},{24,8},{28,12},{1,17},{... | collective-permute-start | bytes 1032200 | tf_op jit(solution)/shard_map/ppermute | solution.py:42
  244.5 25.6 %collective-permute-start.41 = (bf16[192,896]{1,0:T(8,128)(2,1)S(1)}, bf16[192,896]{1,0:T(8,128)(2,1)S(1)}, u32[]{:S(2)}, u32[]{:S(2)}) collective-permute-start(bf16[192,896]{1,0:T(8,128)(2,1)S(1)} %gate_up.5), channel_id=1, source_target_pairs={{0,16},{4,20},{8,24},{12,28},{16,0},{20,4},{24,8},{28,12},{1,17},{... | collective-permute-start | bytes 1032200 | tf_op jit(solution)/shard_map/ppermute | solution.py:42
  279.2 25.7 %collective-permute-start.43 = (bf16[48,3584]{1,0:T(8,128)(2,1)S(1)}, bf16[48,3584]{1,0:T(8,128)(2,1)S(1)}, u32[]{:S(2)}, u32[]{:S(2)}) collective-permute-start(bf16[48,3584]{1,0:T(8,128)(2,1)S(1)} %get-tuple-element.61), channel_id=1, source_target_pairs={{0,2},{1,3},{2,0},{3,1},{4,6},{5,7},{6,4},{7,5},{8,10},{9,11},{10,... | collective-permute-start | bytes 1032200 | tf_op jit(solution)/shard_map/ppermute | solution.py:37
  279.8 25.2 %collective-permute-start.44 = (bf16[48,3584]{1,0:T(8,128)(2,1)S(1)}, bf16[48,3584]{1,0:T(8,128)(2,1)S(1)}, u32[]{:S(2)}, u32[]{:S(2)}) collective-permute-start(bf16[48,3584]{1,0:T(8,128)(2,1)S(1)} %get-tuple-element.62), channel_id=1, source_target_pairs={{0,3},{1,2},{2,1},{3,0},{4,7},{5,6},{6,5},{7,4},{8,11},{9,10},{10,... | collective-permute-start | bytes 1032200 | tf_op jit(solution)/shard_map/ppermute | solution.py:37
  282.6 25.8 %collective-permute-start.54 = (bf16[48,3584]{1,0:T(8,128)(2,1)S(1)}, bf16[48,3584]{1,0:T(8,128)(2,1)S(1)}, u32[]{:S(2)}, u32[]{:S(2)}) collective-permute-start(bf16[48,3584]{1,0:T(8,128)(2,1)S(1)} %out_norm.3.refs_0_), channel_id=1, source_target_pairs={{0,3},{1,2},{2,1},{3,0},{4,7},{5,6},{6,5},{7,4},{8,11},{9,10},{10,... | collective-permute-start | bytes 1032200 | tf_op jit(solution)/shard_map/ppermute | solution.py:37
  283.3 36.4 %collective-permute-start.53 = (bf16[48,3584]{1,0:T(8,128)(2,1)S(1)}, bf16[48,3584]{1,0:T(8,128)(2,1)S(1)}, u32[]{:S(2)}, u32[]{:S(2)}) collective-permute-start(bf16[48,3584]{1,0:T(8,128)(2,1)S(1)} %out_norm.3.refs_0_), channel_id=1, source_target_pairs={{0,2},{1,3},{2,0},{3,1},{4,6},{5,7},{6,4},{7,5},{8,10},{9,11},{10,... | collective-permute-start | bytes 1032200 | tf_op jit(solution)/shard_map/ppermute | solution.py:37
  289.6 30.1 %collective-permute-start.52 = (bf16[48,3584]{1,0:T(8,128)(2,1)S(1)}, bf16[48,3584]{1,0:T(8,128)(2,1)S(1)}, u32[]{:S(2)}, u32[]{:S(2)}) collective-permute-start(bf16[48,3584]{1,0:T(8,128)(2,1)S(1)} %out_norm.3.refs_0_), channel_id=1, source_target_pairs={{0,1},{1,0},{2,3},{3,2},{4,5},{5,4},{6,7},{7,6},{8,9},{9,8},{10,11... | collective-permute-start | bytes 1032200 | tf_op jit(solution)/shard_map/ppermute | solution.py:37
  (88 other events, 708.1 us)
